TPU v7x, 256 devices: a whole 4x4x8 slice. The times are simulated.
256 devices in a mesh: member: 32 (over z, y), slab: 8 (over x, core).
Axes of the slice: x: 4, y: 4, z: 8, core: 2. Of those that a mesh axis runs over, the one named last changes fastest.
Arguments:
- members: bfloat16 [64, 256, 8192], P('member', 'slab'), may hold values from -6 to 6
- direction: float32 [256, 8192], P('slab'), may hold values from -100 to 100
- residual: float32 [256, 8192], P('slab', 'member'), may hold values from -100 to 100
- iterate: float32 [256, 8192], P('slab', 'member'), may hold values from -6 to 6
- tiles: bfloat16 [64, 4, 128, 128], replicated, may hold values from -0.25 to 0.25
- columns: int32 [64, 4], replicated, may hold values from 0 to 63, as said below
- vertical: float32 [256, 9], replicated, may hold values from -2 to 2
Outputs:
- iterate_new: float32 [256, 8192], P('slab', 'member')
- residual_new: float32 [256, 8192], P('slab', 'member')
- direction_new: float32 [256, 8192], P('slab', 'member')
Inputs may be any that keep to these rules, and one draw needn't show every extreme that they name: `columns`: row block r lists 4 distinct column blocks, r itself first.
All inputs are finite; a program needn't handle non-finite values.
Results may differ from a plain program's by a relative error of at most 0.00087.
Values may be sent and summed in bfloat16 or wider, within the bound.
No kernel may reach another device: no remote copies, remote signals or barrier semaphores. Data moves between devices by JAX's collectives and lax.ppermute only.
A program may use at most 64 MiB of HBM per device.

v0:
```python
import jax
import jax.numpy as jnp
from jax import lax
from jax.sharding import PartitionSpec as P

REACH = 4


def padded(block, sides, width):
    for axis, dim in sides:
        count = lax.axis_size(axis)
        forward = [(i, i + 1) for i in range(count - 1)]
        backward = [(target, source) for source, target in forward]
        low = lax.ppermute(
            lax.slice_in_dim(block, block.shape[dim] - width, None, axis=dim), axis, forward
        )
        high = lax.ppermute(lax.slice_in_dim(block, 0, width, axis=dim), axis, backward)
        block = jnp.concatenate([low, block, high], axis=dim)
    return block


def on_device(members, direction, residual, iterate, tiles, columns, vertical):
    mem_dev, lev_dev, points = members.shape
    blocks, per_row, tile = (tiles.shape[0], tiles.shape[1], tiles.shape[2])
    vectors = mem_dev * lev_dev
    share = points // lax.axis_size("member")
    level_start = lax.axis_index("slab") * lev_dev
    wide_members = members.astype(jnp.float32)
    mixed = (wide_members * direction[None]).astype(jnp.bfloat16).reshape(vectors, blocks, tile)
    spread = jnp.einsum("vra,rjab->jvrb", mixed, tiles, preferred_element_type=jnp.float32)
    back = jnp.zeros((vectors, blocks, tile), jnp.float32)
    for column_slot in range(per_row):
        back = back.at[:, columns[:, column_slot], :].add(spread[column_slot])
    back = back.astype(jnp.bfloat16).reshape(mem_dev, lev_dev, points)
    rimmed = padded(back, (("slab", 1),), REACH)
    padded_band = jnp.pad(vertical, ((REACH, REACH), (0, 0)))
    local_band = lax.dynamic_slice_in_dim(padded_band, level_start, lev_dev + 2 * REACH, 0)
    adjoint = jnp.zeros((mem_dev, lev_dev, points), jnp.float32)
    for offset in range(2 * REACH + 1):
        start = 2 * REACH - offset
        adjoint = adjoint + local_band[start : start + lev_dev, offset][None, :, None] * rimmed[
            :, start : start + lev_dev, :
        ].astype(jnp.float32)
    lifted = adjoint.astype(jnp.bfloat16).reshape(vectors, blocks, tile)
    picked = lifted[:, columns]
    forward = jnp.einsum("vrjb,rjab->vra", picked, tiles, preferred_element_type=jnp.float32)
    forward = forward.astype(jnp.bfloat16).reshape(mem_dev, lev_dev, points)
    rimmed_next = padded(forward, (("slab", 1),), REACH)
    own_band = lax.dynamic_slice_in_dim(vertical, level_start, lev_dev, 0)
    smoothed = jnp.zeros((mem_dev, lev_dev, points), jnp.float32)
    for offset in range(2 * REACH + 1):
        smoothed = smoothed + own_band[:, offset][None, :, None] * rimmed_next[
            :, offset : offset + lev_dev, :
        ].astype(jnp.float32)
    partial_value = jnp.sum(wide_members * smoothed, axis=0)
    column_start = lax.axis_index("member") * share
    summed = lax.psum(partial_value, "member")
    total = lax.dynamic_slice_in_dim(summed, column_start, share, 1)
    own_direction = lax.dynamic_slice_in_dim(direction, column_start, share, 1)
    member_count = mem_dev * lax.axis_size("member")
    image = own_direction + total / (member_count - 1)
    norm_old, curvature = lax.psum(
        (jnp.sum(residual * residual), jnp.sum(own_direction * image)), ("member", "slab")
    )
    alpha = norm_old / curvature
    residual_new = residual - alpha * image
    norm_new = lax.psum(jnp.sum(residual_new * residual_new), ("member", "slab"))
    iterate_new = iterate + alpha * own_direction
    direction_new = residual_new + norm_new / norm_old * own_direction
    return (iterate_new, residual_new, direction_new)


def solution(mesh):
    placed = (
        P("member", "slab", None),
        P("slab", None),
        P("slab", "member"),
        P("slab", "member"),
        P(),
        P(),
        P(),
    )
    return jax.shard_map(
        on_device,
        mesh=mesh,
        in_specs=placed,
        out_specs=(P("slab", "member"), P("slab", "member"), P("slab", "member")),
        check_vma=False,
    )
```

profile of v0, /device:TPU:1, one launch (start us, length us, event | category | flops | bytes accessed | tf_op | source)
XLA Modules:
  0.0 398.6 jit_solution(1685791330020815833)
XLA Ops:
  7.2 0.0 all-reduce.4.cloned.1.call-start
  7.2 1.7 fusion
  8.9 0.3 copy.24
  9.2 5.4 %convolution_bitcast_fusion = f32[4,64,64,128]{3,1,0,2:T(8,128)S(1)} fusion(bf16[64,4,128,128]{3,2,1,0:T(8,128)(2,1)} %param.11, bf16[64,64,128,1]{2,1,0,3:T(8,128)(2,1)S(1)} %bitcast.84), kind=kOutput, calls=%fused_computation.5 | convolution fusion | flops 536870912 | bytes 17825792 | tf_op jit(solution)/shard_map/vra,rjab->jvrb/dot_general | solution.py:30
  14.6 0.0 copy-start.5
  14.6 3.4 slice_bitcast_fusion
  18.0 0.0 copy-done.5
  18.0 0.2 broadcast_in_dim.4
  18.2 7.0 %scatter_fusion = f32[64,64,128]{2,0,1:T(8,128)S(1)} fusion(f32[64,64,128]{2,0,1:T(8,128)S(1)} %broadcast_in_dim.4, s32[64]{0:T(128)S(1)} %get-tuple-element.38, f32[64,64,128]{2,1,0:T(8,128)} %get-tuple-element.10), kind=kCustom, calls=%fused_computation.1 | custom fusion | flops 524288 | bytes 6291712 | tf_op jit(solution)/shard_map/scatter-add | solution.py:33
  25.3 7.0 %scatter_fusion.1 = f32[64,64,128]{2,0,1:T(8,128)S(1)} fusion(f32[64,64,128]{2,0,1:T(8,128)S(1)} %scatter_fusion, s32[64]{0:T(128)S(1)} %get-tuple-element.37, f32[64,64,128]{2,1,0:T(8,128)} %get-tuple-element.9), kind=kCustom, calls=%fused_computation.2 | custom fusion | flops 524288 | bytes 6291712 | tf_op jit(solution)/shard_map/scatter-add | solution.py:33
  32.3 7.0 %scatter_fusion.2 = f32[64,64,128]{2,0,1:T(8,128)S(1)} fusion(f32[64,64,128]{2,0,1:T(8,128)S(1)} %scatter_fusion.1, s32[64]{0:T(128)S(1)} %get-tuple-element.36, f32[64,64,128]{2,1,0:T(8,128)} %get-tuple-element.8), kind=kCustom, calls=%fused_computation.3 | custom fusion | flops 524288 | bytes 6291712 | tf_op jit(solution)/shard_map/scatter-add | solution.py:33
  39.3 7.0 %scatter_fusion.3 = f32[64,64,128]{2,0,1:T(8,128)S(1)} fusion(f32[64,64,128]{2,0,1:T(8,128)S(1)} %scatter_fusion.2, s32[64]{0:T(128)S(1)} %get-tuple-element.35, f32[64,64,128]{2,1,0:T(8,128)} %get-tuple-element.7), kind=kCustom, calls=%fused_computation.4 | custom fusion | flops 524288 | bytes 6291712 | tf_op jit(solution)/shard_map/scatter-add | solution.py:33
  46.3 0.2 convert_element_type.76
  46.5 0.7 copy.16
  47.2 0.0 copy-start.3
  47.2 0.5 reshape.38
  47.7 0.1 fusion.25
  47.8 5.2 %collective-permute-start = (bf16[2,4,8192]{2,1,0:T(4,128)(2,1)S(1)}, bf16[2,4,8192]{2,1,0:T(4,128)(2,1)S(1)}, u32[]{:S(2)}, u32[]{:S(2)}) collective-permute-start(bf16[2,4,8192]{2,1,0:T(4,128)(2,1)S(1)} %get-tuple-element.15), channel_id=1, source_target_pairs={{1,0},{2,1},{3,2},{4,3},{5,4},{6,5},{7,6},{9,8},{10,9},{11,10},{12... | collective-permute-start | bytes 393224 | tf_op jit(solution)/shard_map/ppermute | solution.py:17
  53.0 2.1 collective-permute-start.1
  55.1 0.1 constant_dynamic-update-slice_fusion.1
  55.2 0.1 copy.17
  55.3 0.1 reshape.43
  55.4 0.0 copy-done.3
  55.4 0.1 dynamic-slice_bitcast_fusion.2
  55.5 0.1 fusion.10
  55.7 0.0 collective-permute-done
  55.7 0.1 constant_dynamic-update-slice_fusion
  55.8 1.1 collective-permute-done.1
  56.8 2.8 add_convert_fusion
  59.6 0.3 copy.25
  59.9 0.7 copy.18
  60.6 3.0 gather_fusion
  63.6 7.6 %fusion.2 = bf16[64,64,128]{2,0,1:T(8,128)(2,1)S(1)} fusion(bf16[64,64,4,128]{3,0,2,1:T(8,128)(2,1)} %bitcast.83, bf16[64,4,128,128]{3,2,1,0:T(8,128)(2,1)} %param.11), kind=kOutput, calls=%fused_computation.22 | convolution fusion | flops 537395200 | bytes 13631488 | tf_op jit(solution)/shard_map/vrjb,rjab->vra/dot_general | solution.py:46
  71.2 0.7 copy.19
  71.9 0.0 copy-start
  71.9 0.5 reshape.40
  72.4 0.1 fusion.24
  72.5 1.9 collective-permute-start.3
  74.5 0.1 constant_dynamic-update-slice_fusion.3
  74.6 4.4 %collective-permute-start.2 = (bf16[2,4,8192]{2,1,0:T(4,128)(2,1)S(1)}, bf16[2,4,8192]{2,1,0:T(4,128)(2,1)S(1)}, u32[]{:S(2)}, u32[]{:S(2)}) collective-permute-start(bf16[2,4,8192]{2,1,0:T(4,128)(2,1)S(1)} %get-tuple-element.14), channel_id=1, source_target_pairs={{0,1},{1,2},{2,3},{3,4},{4,5},{5,6},{6,7},{8,9},{9,10},{10,11},{11... | collective-permute-start | bytes 393224 | tf_op jit(solution)/shard_map/ppermute | solution.py:14
  78.9 0.6 collective-permute-done.3
  79.5 0.1 constant_dynamic-update-slice_fusion.2
  79.6 1.2 collective-permute-done.2
  80.8 0.0 copy-done
  80.8 0.0 copy-start.2
  80.8 0.0 copy-start.4
  80.8 4.1 %fusion.1 = f32[32,8192]{1,0:T(8,128)} fusion(bf16[2,32,8192]{2,1,0:T(8,128)(2,1)S(1)} %copy-done, bf16[2,32,8192]{2,1,0:T(8,128)(2,1)S(1)} %reshape.40, bf16[2,4,8192]{2,1,0:T(4,128)(2,1)S(1)} %collective-permute-done.2, bf16[2,36,8192]{2,1,0:T(8,128)(2,1)S(1)} %constant_dynamic-update-slice_fusion.2, f32[32]{0:T(128)S(1)} %get-tuple-element.34, ...), kind=kLoop, calls=%fused_computation.15 | loop fusion | flops 21233664 | bytes 7472256 | tf_op jit(solution)/shard_map/reduce_sum | solution.py:55
  85.0 0.0 all-reduce.4.cloned.1.call-update
  85.0 0.0 copy-done.2
  85.0 0.6 multiply_reduce_fusion.2
  85.6 147.5 %all-reduce.4.cloned.1.call-done = f32[32,8192]{1,0:T(8,128)} async-done(((f32[32,8192]{1,0:T(8,128)}), f32[32,8192]{1,0:T(8,128)}) %all-reduce.4.cloned.1.call-update) | async-done | bytes 1048592 | tf_op jit(solution)/shard_map/psum | solution.py:57
  233.1 1.4 multiply_reduce_fusion.1
  234.5 79.0 %all-reduce.1 = (f32[]{:T(128)}, f32[]{:T(128)}) all-reduce(f32[]{:T(128)} %multiply_reduce_fusion.2, f32[]{:T(128)} %multiply_reduce_fusion.1), channel_id=1, replica_groups=mesh['member'=32,'slab'=8] {'member','slab'}, use_global_device_ids=true, to_apply=%region_1.0 | all-reduce | flops 2 | bytes 16 | tf_op jit(solution)/shard_map/psum | solution.py:62
  314.8 1.4 multiply_reduce_fusion
  316.2 0.0 copy-start.1
  316.2 72.8 %psum.31 = f32[]{:T(128)} all-reduce(f32[]{:T(128)} %get-tuple-element.5), channel_id=1, replica_groups=mesh['member'=32,'slab'=8] {'member','slab'}, use_global_device_ids=true, to_apply=%region_11.12 | all-reduce | flops 1 | bytes 8 | tf_op jit(solution)/shard_map/psum | solution.py:67
  390.3 0.0 copy-done.4
  390.4 1.4 multiply_add_fusion
  391.7 0.0 copy-done.1
  (3 shorter events, 0.0 us)
Async XLA Ops:
  7.2 225.9 %all-reduce.4.cloned.1.call-start = ((), (), s32[]{:S(2)}) async-start(), calls=%async_computation | async-start | bytes 2097152 | tf_op jit(solution)/shard_map/psum | solution.py:57
  14.6 3.4 copy-start.5
  47.2 8.2 %copy-start.3 = (f32[256,9]{0,1:T(8,128)S(1)}, f32[256,9]{0,1:T(8,128)}, u32[]{:S(2)}) copy-start(f32[256,9]{0,1:T(8,128)} %param.13) | copy-start | bytes 27652
  47.8 7.8 %collective-permute-start = (bf16[2,4,8192]{2,1,0:T(4,128)(2,1)S(1)}, bf16[2,4,8192]{2,1,0:T(4,128)(2,1)S(1)}, u32[]{:S(2)}, u32[]{:S(2)}) collective-permute-start(bf16[2,4,8192]{2,1,0:T(4,128)(2,1)S(1)} %get-tuple-element.15), channel_id=1, source_target_pairs={{1,0},{2,1},{3,2},{4,3},{5,4},{6,5},{7,6},{9,8},{10,9},{11,10},{12... | collective-permute-start | bytes 393224 | tf_op jit(solution)/shard_map/ppermute | solution.py:17
  53.0 3.9 collective-permute-start.1
  71.9 8.9 %copy-start = (bf16[2,32,8192]{2,1,0:T(8,128)(2,1)S(1)}, bf16[2,32,8192]{2,1,0:T(8,128)(2,1)}, u32[]{:S(2)}) copy-start(bf16[2,32,8192]{2,1,0:T(8,128)(2,1)} %param.7) | copy-start | bytes 3145732
  72.5 7.0 %collective-permute-start.3 = (bf16[2,4,8192]{2,1,0:T(4,128)(2,1)S(1)}, bf16[2,4,8192]{2,1,0:T(4,128)(2,1)S(1)}, u32[]{:S(2)}, u32[]{:S(2)}) collective-permute-start(bf16[2,4,8192]{2,1,0:T(4,128)(2,1)S(1)} %get-tuple-element.13), channel_id=1, source_target_pairs={{1,0},{2,1},{3,2},{4,3},{5,4},{6,5},{7,6},{9,8},{10,9},{11,10},{12... | collective-permute-start | bytes 393224 | tf_op jit(solution)/shard_map/ppermute | solution.py:17
  74.6 6.3 %collective-permute-start.2 = (bf16[2,4,8192]{2,1,0:T(4,128)(2,1)S(1)}, bf16[2,4,8192]{2,1,0:T(4,128)(2,1)S(1)}, u32[]{:S(2)}, u32[]{:S(2)}) collective-permute-start(bf16[2,4,8192]{2,1,0:T(4,128)(2,1)S(1)} %get-tuple-element.14), channel_id=1, source_target_pairs={{0,1},{1,2},{2,3},{3,4},{4,5},{5,6},{6,7},{8,9},{9,10},{10,11},{11... | collective-permute-start | bytes 393224 | tf_op jit(solution)/shard_map/ppermute | solution.py:14
  80.8 4.2 %copy-start.2 = (f32[32,256]{1,0:T(8,128)S(1)}, f32[32,256]{1,0:T(8,128)}, u32[]{:S(2)}) copy-start(f32[32,256]{1,0:T(8,128)} %param.9) | copy-start | bytes 98308
  80.8 309.5 %copy-start.4 = (f32[32,256]{1,0:T(8,128)S(1)}, f32[32,256]{1,0:T(8,128)}, u32[]{:S(2)}) copy-start(f32[32,256]{1,0:T(8,128)} %param.10) | copy-start | bytes 98308
  316.2 75.6 %copy-start.1 = (f32[32,256]{1,0:T(8,128)}, f32[32,256]{1,0:T(8,128)S(1)}, u32[]{:S(2)}) copy-start(f32[32,256]{1,0:T(8,128)S(1)} %get-tuple-element.6) | copy-start | bytes 98308
Sparse Core Ops, SparseCore 0:
  85.1 147.9 all-reduce.3
where the time goes:
time: 400 us; the launch traced here: 399 us
  blocking collectives  152 us (38%)
  waiting for transfers between devices  150 us (38%)
  other arithmetic  41.7 us (10%)
  between operations  17 us (4%)
  starting transfers between devices  13.6 us (3%)
  matrix products  13 us (3%)
  local copies, waits for them, and re-layouts  11.2 us (3%)
    psum x1, waiting for transfers between devices, on_device(): summed = lax.psum(partial_value, 'member')  147 us
    psum x1, blocking collectives, on_device(): lax.psum((jnp.sum(residual * residual), jnp.sum(own_direction * image)),...  79 us
    psum x1, blocking collectives, on_device(): lax.psum(jnp.sum(residual_new * residual_new), ('member', 'slab'))  72.8 us
    scatter-add x4, other arithmetic, on_device(): back = back.at[:, columns[:, column_slot], :].add(spread[column_slot])  28 us
  transfers between devices with their start and end apart: 5, of which 4 were waited for; matrix products, arithmetic and copies ran while one was open for 0% of the time, Pallas kernels for 0%

commit v1 on v0

v1 whole, which is shorter than its diff:
```python
import jax
import jax.numpy as jnp
from jax import lax
from jax.experimental import pallas as pl
from jax.experimental.pallas import tpu as pltpu
from jax.sharding import PartitionSpec as P

REACH = 4
HALO = 2 * REACH
CHUNKS = 16
F32 = jnp.float32
BF16 = jnp.bfloat16
NT = (((1,), (1,)), ((), ()))


def split3(value):
    high = value.astype(BF16)
    rest = value - high.astype(F32)
    middle = rest.astype(BF16)
    low = (rest - middle.astype(F32)).astype(BF16)
    return jnp.concatenate([high, middle, low], axis=0)


def product_kernel(
    columns_ref, band_ref, members_ref, direction_ref, below_ref, above_ref, tiles_hbm,
    out_ref, tiles_ref, smooth_ref, acc_ref, back_ref, sems,
):
    mem_dev, lev_dev, points = members_ref.shape
    blocks, per_row, tile, _ = tiles_ref.shape
    vectors = mem_dev * lev_dev
    part = blocks // CHUNKS

    def fetch(i):
        rows = pl.ds(i * part, part)
        return pltpu.make_async_copy(tiles_hbm.at[rows], tiles_ref.at[rows], sems.at[i])

    for i in range(CHUNKS):
        fetch(i).start()

    band = split3(band_ref[...])
    acc_ref[...] = jnp.zeros_like(acc_ref)

    def vertical_step(g, carry):
        cols = pl.ds(pl.multiple_of(g * 2 * tile, 2 * tile), 2 * tile)
        field = direction_ref[:, cols]
        mixed = [(members_ref[m, :, cols].astype(F32) * field).astype(BF16) for m in range(mem_dev)]
        stacked = jnp.concatenate(mixed + [below_ref[:, cols], above_ref[:, cols]], axis=0)
        three = jnp.dot(band, stacked, preferred_element_type=F32)
        total = (three[2 * vectors :] + three[vectors : 2 * vectors]) + three[:vectors]
        total = total.astype(BF16)
        smooth_ref[2 * g] = total[:, :tile]
        smooth_ref[2 * g + 1] = total[:, tile:]
        return carry

    lax.fori_loop(0, blocks // 2, vertical_step, 0, unroll=2)

    def adjoint_step(r, carry):
        left = smooth_ref[r]
        where = [columns_ref[r * per_row + j] for j in range(per_row)]
        old = [acc_ref[c] for c in where]
        new = [
            old[j] + jnp.dot(left, tiles_ref[r, j], preferred_element_type=F32)
            for j in range(per_row)
        ]
        for j in range(per_row):
            acc_ref[where[j]] = new[j]
        return carry

    for i in range(CHUNKS):
        fetch(i).wait()
        lax.fori_loop(i * part, (i + 1) * part, adjoint_step, 0, unroll=4)

    back_ref[...] = acc_ref[...].astype(BF16)

    def forward_row(r):
        left = jnp.concatenate(
            [back_ref[columns_ref[r * per_row + j]] for j in range(per_row)], axis=1
        )
        right = jnp.concatenate([tiles_ref[r, j] for j in range(per_row)], axis=1)
        field = lax.dot_general(left, right, NT, preferred_element_type=F32)
        cols = pl.ds(pl.multiple_of(r * tile, tile), tile)
        total = jnp.zeros((lev_dev, tile), F32)
        for m in range(mem_dev):
            total = total + members_ref[m, :, cols].astype(F32) * field[m * lev_dev : (m + 1) * lev_dev]
        return total

    wide = out_ref.shape[2] // tile

    def forward_step(g, carry):
        for k in range(wide):
            out_ref[g, :, k * tile : (k + 1) * tile] = forward_row(g * wide + k).astype(out_ref.dtype)
        return carry

    lax.fori_loop(0, blocks // wide, forward_step, 0, unroll=2)


def two_sum(a, b):
    s = a + b
    t = s - a
    return s, (a - (s - t)) + (b - t)


def two_product(a, b):
    def halves(x):
        t = 4097.0 * x
        high = t - (t - x)
        return high, x - high

    p = a * b
    ah, al = halves(a)
    bh, bl = halves(b)
    return p, ((ah * bh - p) + ah * bl + al * bh) + al * bl


def add_pairs(a, b):
    s, e = two_sum(a[0], b[0])
    return two_sum(s, e + (a[1] + b[1]))


def sum_pairs(pairs):
    while len(pairs) > 1:
        rest = pairs[len(pairs) // 2 * 2 :]
        pairs = [add_pairs(pairs[i], pairs[i + 1]) for i in range(0, len(pairs) - 1, 2)] + rest
    return pairs[0]


def rows_of(pair):
    return [(pair[0][i : i + 1], pair[1][i : i + 1]) for i in range(pair[0].shape[0])]


def dot_pairs(a, b):
    pair = two_product(a, b)
    lanes = a.shape[1]
    pieces = [
        (pair[0][i : i + 8, j : j + 128], pair[1][i : i + 8, j : j + 128])
        for i in range(0, a.shape[0], 8)
        for j in range(0, lanes, 128)
    ]
    return sum_pairs(rows_of(sum_pairs(pieces)))


def image_kernel(share_ref, parts_ref, direction_ref, residual_ref, image_ref, sums_ref, *, scale):
    total = parts_ref[0].astype(F32)
    for i in range(1, parts_ref.shape[0]):
        total = total + parts_ref[i].astype(F32)
    own = direction_ref[...]
    residual = residual_ref[...]
    image = own + total / scale
    image_ref[...] = image
    rr = dot_pairs(residual, residual)
    ri = dot_pairs(residual, image)
    ii = dot_pairs(image, image)
    di = dot_pairs(own, image)
    sums_ref[...] = jnp.concatenate([rr[0], rr[1], ri[0], ri[1], ii[0], ii[1], di[0], di[1]], axis=0)


def add_devices(parts_ref):
    pairs = []
    for k in range(4):
        pairs.append(
            sum_pairs(
                [(parts_ref[i, 2 * k : 2 * k + 1], parts_ref[i, 2 * k + 1 : 2 * k + 2]) for i in range(parts_ref.shape[0])]
            )
        )
    return pairs


def gather_kernel(parts_ref, out_ref):
    out_ref[...] = jnp.concatenate([x for pair in add_devices(parts_ref) for x in pair], axis=0)


def update_kernel(share_ref, parts_ref, direction_ref, residual_ref, iterate_ref, image_ref, x_ref, r_ref, d_ref):
    pairs = add_devices(parts_ref)
    lanes = 128
    while lanes > 1:
        lanes //= 2
        pairs = [add_pairs((h[:, :lanes], l[:, :lanes]), (h[:, lanes:], l[:, lanes:])) for h, l in pairs]
    rr, ri, ii, di = pairs
    norm_old = rr[0] + rr[1]
    alpha = norm_old / (di[0] + di[1])

    def scaled(pair):
        p, e = two_product(pair[0], alpha)
        return p, e + pair[1] * alpha

    inner = add_pairs(scaled(ii), (-2.0 * ri[0], -2.0 * ri[1]))
    norm_new = add_pairs(rr, scaled(inner))
    beta = (norm_new[0] + norm_new[1]) / norm_old
    own = direction_ref[...]
    residual_new = residual_ref[...] - alpha * image_ref[...]
    x_ref[...] = iterate_ref[...] + alpha * own
    r_ref[...] = residual_new
    d_ref[...] = residual_new + beta * own


def gathered(value, axis):
    count = lax.axis_size(axis)
    return lax.all_to_all(
        jnp.broadcast_to(value[None], (count,) + value.shape), axis, 0, 0, tiled=True
    )


def level_matrix(vertical, level_start, lev_dev, mem_dev):
    levels = vertical.shape[0]
    span = lev_dev + 2 * HALO
    padded = jnp.pad(vertical, ((HALO, HALO), (0, 0)))
    band = lax.dynamic_slice_in_dim(padded, level_start, span, 0)
    width = span + 2 * REACH
    row = lax.broadcasted_iota(jnp.int32, (span, width), 0)
    col = lax.broadcasted_iota(jnp.int32, (span, width), 1)
    level = col + (level_start - HALO - REACH)
    dense = jnp.zeros((span, width), F32)
    for offset in range(2 * REACH + 1):
        dense = jnp.where(col == row + offset, band[:, offset : offset + 1], dense)
    dense = jnp.where((level >= 0) & (level < levels), dense, 0.0)
    both = jnp.einsum("lq,kq->lk", dense[HALO : HALO + lev_dev], dense, precision=lax.Precision.HIGHEST)
    own, low, high = both[:, HALO : HALO + lev_dev], both[:, :HALO], both[:, HALO + lev_dev :]
    eye = jnp.eye(mem_dev, dtype=F32)
    return jnp.concatenate([jnp.kron(eye, own), jnp.kron(eye, low), jnp.kron(eye, high)], axis=1)


def on_device(members, direction, residual, iterate, tiles, columns, vertical):
    mem_dev, lev_dev, points = members.shape
    blocks, per_row, tile = tiles.shape[:3]
    vectors = mem_dev * lev_dev
    groups = lax.axis_size("member")
    share = points // groups
    slabs = lax.axis_size("slab")
    member_count = mem_dev * groups
    level_start = lax.axis_index("slab") * lev_dev

    def edge(start):
        mixed = members[:, start : start + HALO].astype(F32) * direction[None, start : start + HALO]
        return mixed.astype(BF16).reshape(mem_dev * HALO, points)

    upward = [(i, i + 1) for i in range(slabs - 1)]
    downward = [(target, source) for source, target in upward]
    below = lax.ppermute(edge(lev_dev - HALO), "slab", upward)
    above = lax.ppermute(edge(0), "slab", downward)
    band = level_matrix(vertical, level_start, lev_dev, mem_dev)

    vmem = pl.BlockSpec(memory_space=pltpu.VMEM)
    smem = pl.BlockSpec(memory_space=pltpu.SMEM)
    partial_value = pl.pallas_call(
        product_kernel,
        out_shape=jax.ShapeDtypeStruct((groups, lev_dev, share), BF16),
        in_specs=[smem, vmem, vmem, vmem, vmem, vmem, pl.BlockSpec(memory_space=pl.ANY)],
        out_specs=vmem,
        scratch_shapes=[
            pltpu.VMEM(tiles.shape, BF16),
            pltpu.VMEM((blocks, vectors, tile), BF16),
            pltpu.VMEM((blocks, vectors, tile), F32),
            pltpu.VMEM((blocks, vectors, tile), BF16),
            pltpu.SemaphoreType.DMA((CHUNKS,)),
        ],
        compiler_params=pltpu.CompilerParams(vmem_limit_bytes=40 * 2**20),
        name="product",
    )(columns.reshape(-1), band, members, direction, below, above, tiles)

    parts = lax.all_to_all(partial_value, "member", 0, 0, tiled=True)
    me = lax.axis_index("member").reshape(1)
    whole = lambda shape: pl.BlockSpec(shape, lambda i, s: (0,) * len(shape))
    own = pl.BlockSpec((lev_dev, share), lambda i, s: (0, s[0]))
    field = jax.ShapeDtypeStruct((lev_dev, share), F32)
    square = whole((lev_dev, share))
    image, sums = pl.pallas_call(
        lambda *refs: image_kernel(*refs, scale=float(member_count - 1)),
        out_shape=(field, jax.ShapeDtypeStruct((8, 128), F32)),
        grid_spec=pltpu.PrefetchScalarGridSpec(
            num_scalar_prefetch=1,
            grid=(1,),
            in_specs=[whole((groups, lev_dev, share)), own, square],
            out_specs=(square, whole((8, 128))),
        ),
        name="image",
    )(me, parts, direction, residual)

    first = gathered(sums, "slab")
    middle = pl.pallas_call(
        gather_kernel, out_shape=jax.ShapeDtypeStruct((8, 128), F32), in_specs=[vmem], out_specs=vmem, name="gather"
    )(first)
    second = gathered(middle, "member")
    return pl.pallas_call(
        update_kernel,
        out_shape=(field, field, field),
        grid_spec=pltpu.PrefetchScalarGridSpec(
            num_scalar_prefetch=1,
            grid=(1,),
            in_specs=[whole((groups, 8, 128)), own, square, square, square],
            out_specs=(square, square, square),
        ),
        name="update",
    )(me, second, direction, residual, iterate, image)


def solution(mesh):
    placed = (
        P("member", "slab", None),
        P("slab", None),
        P("slab", "member"),
        P("slab", "member"),
        P(),
        P(),
        P(),
    )
    return jax.shard_map(
        on_device,
        mesh=mesh,
        in_specs=placed,
        out_specs=(P("slab", "member"), P("slab", "member"), P("slab", "member")),
        check_vma=False,
    )
```

time: 400 us -> 96.6 us (0.24)
  waiting for transfers between devices: 150 us -> 17.1 us
  blocking collectives: 152 us -> 25.3 us
  other arithmetic: 41.7 us -> 1.59 us
  Pallas kernels: 0 us -> 21.4 us
  between operations: 17 us -> 0.79 us
  matrix products: 13 us -> 0.15 us
  starting transfers between devices: 13.6 us -> 17.7 us
    psum x2 -> x0, blocking collectives: 152 us -> none  [the longest x1 79 us: on_device(): lax.psum((jnp.sum(residual * residual), jnp.sum(own_direction * image)),...]
    psum x1 -> x0, waiting for transfers between devices: 147 us -> none  [on_device(): summed = lax.psum(partial_value, 'member')]
    scatter-add x4 -> x0, other arithmetic: 28 us -> none  [on_device(): back = back.at[:, columns[:, column_slot], :].add(spread[column_slot])]
    all_to_all x0 -> x2, blocking collectives: none -> 25.3 us  [gathered(): lax.all_to_all(jnp.broadcast_to(value[None], (count,) + value.shape), axi...]
    pallas_call x0 -> x4, Pallas kernels: none -> 21.4 us  [the longest x1 14.8 us: on_device(): pl.pallas_call(product_kernel, out_shape=jax.ShapeDtypeStruct((groups, le...]
    all_to_all x0 -> x1, waiting for transfers between devices: none -> 14.9 us  [on_device(): parts = lax.all_to_all(partial_value, 'member', 0, 0, tiled=True)]
    dot_general x2 -> x1, matrix products: 13 us -> 0.15 us  [level_matrix(): jnp.einsum('lq,kq->lk', dense[HALO:HALO + lev_dev], dense, precision=lax....]
    all_to_all x0 -> x1, starting transfers between devices: none -> 11.2 us  [on_device(): parts = lax.all_to_all(partial_value, 'member', 0, 0, tiled=True)]
  transfers between devices with their start and end apart: 5 -> 3, of which waited for: 4 -> 2; matrix products, arithmetic and copies ran while one was open for 0% -> 4% of each run, Pallas kernels for 0% -> 0%
where the time goes in v1:
time: 96.6 us; the launch traced here: 95.9 us
  blocking collectives  25.3 us (26%)
  Pallas kernels  21.4 us (22%)
  starting transfers between devices  17.7 us (18%)
  waiting for transfers between devices  17.1 us (18%)
  local copies, waits for them, and re-layouts  11.9 us (12%)
  other arithmetic  1.59 us (2%)
    all_to_all x2, blocking collectives, gathered(): lax.all_to_all(jnp.broadcast_to(value[None], (count,) + value.shape), axi...  25.3 us
    all_to_all x1, waiting for transfers between devices, on_device(): parts = lax.all_to_all(partial_value, 'member', 0, 0, tiled=True)  14.9 us
    pallas_call x1, Pallas kernels, on_device(): pl.pallas_call(product_kernel, out_shape=jax.ShapeDtypeStruct((groups, le...  14.8 us
    all_to_all x1, starting transfers between devices, on_device(): parts = lax.all_to_all(partial_value, 'member', 0, 0, tiled=True)  11.2 us
    unnamed x9, local copies, waits for them, and re-layouts  7.39 us
    ppermute x1, starting transfers between devices, on_device(): below = lax.ppermute(edge(lev_dev - HALO), 'slab', upward)  4.51 us
    pallas_call x1, Pallas kernels, on_device(): pl.pallas_call(update_kernel, out_shape=(field, field, field), grid_spec=...  3.33 us
    ppermute x1, waiting for transfers between devices, on_device(): above = lax.ppermute(edge(0), 'slab', downward)  2.23 us
  transfers between devices with their start and end apart: 3, of which 2 were waited for; matrix products, arithmetic and copies ran while one was open for 4% of the time, Pallas kernels for 0%

profile of v1, /device:TPU:1, one launch (start us, length us, event | category | flops | bytes accessed | tf_op | source)
XLA Modules:
  0.0 95.9 jit_solution(10851592973295381107)
XLA Ops:
  0.6 1.1 %fusion.13 = (f32[8,8192]{1,0:T(8,128)S(1)}, f32[8,8192]{1,0:T(8,128)S(1)}) fusion(f32[32,8192]{1,0:T(8,128)} %direction_ref.3), kind=kLoop, calls=%fused_computation.48 | loop fusion | bytes 1048576 | tf_op jit(solution)/shard_map/slice | solution.py:233
  1.7 1.1 %fusion.1 = (bf16[16,8192]{1,0:T(8,128)(2,1)S(1)}, bf16[16,8192]{1,0:T(8,128)(2,1)S(1)}) fusion(f32[8,8192]{1,0:T(8,128)S(1)} %get-tuple-element.9, bf16[2,32,8192]{2,1,0:T(8,128)(2,1)} %members_ref.1, f32[8,8192]{1,0:T(8,128)S(1)} %get-tuple-element.10), kind=kLoop, calls=%fused_computation.3 | loop fusion | flops 786432 | bytes 1572864 | tf_op jit(solution)/shard_map/reshape | solution.py:234
  2.8 4.5 %collective-permute-start = (bf16[16,8192]{1,0:T(8,128)(2,1)S(1)}, bf16[16,8192]{1,0:T(8,128)(2,1)S(1)}, u32[]{:S(2)}, u32[]{:S(2)}) collective-permute-start(bf16[16,8192]{1,0:T(8,128)(2,1)S(1)} %get-tuple-element.8), channel_id=1, source_target_pairs={{0,1},{1,2},{2,3},{3,4},{4,5},{5,6},{6,7},{8,9},{9,10},{10,11},{11... | collective-permute-start | bytes 786440 | tf_op jit(solution)/shard_map/ppermute | solution.py:238
  7.3 1.9 %collective-permute-start.1 = (bf16[16,8192]{1,0:T(8,128)(2,1)S(1)}, bf16[16,8192]{1,0:T(8,128)(2,1)S(1)}, u32[]{:S(2)}, u32[]{:S(2)}) collective-permute-start(bf16[16,8192]{1,0:T(8,128)(2,1)S(1)} %get-tuple-element.7), channel_id=1, source_target_pairs={{1,0},{2,1},{3,2},{4,3},{5,4},{6,5},{7,6},{9,8},{10,9},{11,10},{12... | collective-permute-start | bytes 786440 | tf_op jit(solution)/shard_map/ppermute | solution.py:239
  9.4 1.1 %fusion.5 = (f32[48]{0:T(128)S(1)}, f32[48]{0:T(128)S(1)}, f32[48]{0:T(128)S(1)}, f32[48]{0:T(128)S(1)}, f32[48]{0:T(128)S(1)}, /*index=5*/f32[48]{0:T(128)S(1)}, f32[48]{0:T(128)S(1)}, f32[48]{0:T(128)S(1)}, f32[48]{0:T(128)S(1)}) fusion(s32[]{:T(128)S(6)} %select_n.35, s32[]{:T(128)S(6)} %add.91, f32[256,9]{0,1:T(8,128)} %param.13, s32[]{:T(128)S(6)} %add.98, ...), kind=kLoop, calls=%fused_computation.40 | loop fusion | bytes 10980 | tf_op jit(solution)/shard_map/jit(_where)/broadcast_in_dim | solution.py:214
  10.5 0.2 select_select_fusion
  10.7 0.1 fusion.2
  10.8 0.1 slice.69
  10.9 0.1 fusion.14
  11.0 0.1 copy.11
  11.1 0.1 broadcast_multiply_fusion
  11.2 0.1 mul.88
  11.3 0.1 copy.12
  11.3 0.1 copy.13
  11.4 0.1 broadcast_multiply_fusion.2
  11.5 0.1 mul.92
  11.6 0.1 copy.14
  11.7 0.1 mul.95
  11.7 0.1 copy.15
  11.8 0.8 copy.10
  12.6 0.1 reshape.48.columns_ref
  12.7 0.1 pad_maximum_fusion.band_ref
  12.8 0.0 collective-permute-done.below_ref
  12.8 2.2 %collective-permute-done.1.above_ref = bf16[16,8192]{1,0:T(8,128)(2,1)S(1)} collective-permute-done((bf16[16,8192]{1,0:T(8,128)(2,1)S(1)}, bf16[16,8192]{1,0:T(8,128)(2,1)S(1)}, u32[]{:S(2)}, u32[]{:S(2)}) %collective-permute-start.1) | collective-permute-done | bytes 262176 | tf_op jit(solution)/shard_map/ppermute | solution.py:239
  15.0 0.0 copy-start
  15.0 1.2 %copy-done = f32[32,8192]{1,0:T(8,128)S(1)} copy-done((f32[32,8192]{1,0:T(8,128)S(1)}, f32[32,8192]{1,0:T(8,128)}, u32[]{:S(2)}) %copy-start) | copy-done | bytes 1048600
  16.3 0.0 copy-start.1
  16.3 3.4 %copy-done.1 = bf16[64,4,128,128]{3,2,1,0:T(8,128)(2,1)S(1)} copy-done((bf16[64,4,128,128]{3,2,1,0:T(8,128)(2,1)S(1)}, bf16[64,4,128,128]{3,2,1,0:T(8,128)(2,1)}, u32[]{:S(2)}) %copy-start.1) | copy-done | bytes 8388632
  19.6 0.0 copy-start.2
  19.6 1.2 %copy-done.2 = bf16[2,32,8192]{2,1,0:T(8,128)(2,1)S(1)} copy-done((bf16[2,32,8192]{2,1,0:T(8,128)(2,1)S(1)}, bf16[2,32,8192]{2,1,0:T(8,128)(2,1)}, u32[]{:S(2)}) %copy-start.2) | copy-done | bytes 1048600
  20.9 14.8 %product.1 = bf16[32,32,256]{2,1,0:T(8,128)(2,1)} custom-call(s32[256]{0:T(256)S(1)} %reshape.48.columns_ref, f32[64,96]{1,0:T(8,128)S(1)} %pad_maximum_fusion.band_ref, bf16[2,32,8192]{2,1,0:T(8,128)(2,1)S(1)} %copy-done.2, f32[32,8192]{1,0:T(8,128)S(1)} %copy-done, bf16[16,8192]{1,0:T(8,128)(2,1)S(1)} %collective-permute-done.below_ref, ...), custom_call_target="tpu_custom_call" | custom-call | tf_op jit(solution)/shard_map/product/pallas_call | solution.py:244
  35.7 11.2 %all-to-all-start = ((bf16[32,32,256]{2,1,0:T(8,128)(2,1)}), bf16[32,32,256]{2,1,0:T(8,128)(2,1)S(1)}, u32[]{:S(2)}, u32[]{:S(2)}) async-start(bf16[32,32,256]{2,1,0:T(8,128)(2,1)} %product.1), calls=%async_computation | async-start | bytes 1048576 | tf_op jit(solution)/shard_map/all_to_all | solution.py:260
  46.9 14.9 %all-to-all-done.refs_1_ = bf16[32,32,256]{2,1,0:T(8,128)(2,1)S(1)} async-done(((bf16[32,32,256]{2,1,0:T(8,128)(2,1)}), bf16[32,32,256]{2,1,0:T(8,128)(2,1)S(1)}, u32[]{:S(2)}, u32[]{:S(2)}) %all-to-all-start) | async-done | bytes 524320 | tf_op jit(solution)/shard_map/all_to_all | solution.py:260
  61.8 0.0 copy-start.3
  61.8 0.8 copy-done.3
  62.6 1.9 %image.1 = (f32[32,256]{1,0:T(8,128)}, f32[8,128]{1,0:T(8,128)}) custom-call(s32[1]{0:T(128)} %bitcast.refs_0_.share_ref, bf16[32,32,256]{2,1,0:T(8,128)(2,1)} %copy-done.3, f32[32,8192]{1,0:T(8,128)} %direction_ref.3, f32[32,256]{1,0:T(8,128)} %residual_ref.1), custom_call_target="tpu_custom_call" | custom-call | tf_op jit(solution)/shard_map/image/pallas_call | solution.py:266
  64.5 0.7 broadcast_in_dim.114
  65.2 11.2 %all_to_all.15.parts_ref = f32[8,8,128]{2,1,0:T(8,128)} all-to-all(f32[8,8,128]{2,1,0:T(8,128)S(1)} %broadcast_in_dim.114), channel_id=1, replica_groups=mesh['member'=32,'slab'=8] {'slab'}, dimensions={0} | all-to-all | bytes 65536 | tf_op jit(solution)/shard_map/all_to_all | solution.py:198
  76.4 1.4 %gather.1 = f32[8,128]{1,0:T(8,128)} custom-call(f32[8,8,128]{2,1,0:T(8,128)} %all_to_all.15.parts_ref), custom_call_target="tpu_custom_call" | custom-call | tf_op jit(solution)/shard_map/gather/pallas_call | solution.py:279
  77.8 0.7 broadcast_in_dim.115
  78.5 14.1 %all_to_all.16.parts_ref = f32[32,8,128]{2,1,0:T(8,128)} all-to-all(f32[32,8,128]{2,1,0:T(8,128)S(1)} %broadcast_in_dim.115), channel_id=1, replica_groups=mesh['member'=32,'slab'=8] {'member'}, dimensions={0} | all-to-all | bytes 262144 | tf_op jit(solution)/shard_map/all_to_all | solution.py:198
  92.6 3.3 %update.1 = (f32[32,256]{1,0:T(8,128)}, f32[32,256]{1,0:T(8,128)}, f32[32,256]{1,0:T(8,128)}) custom-call(s32[1]{0:T(128)} %bitcast.refs_0_.share_ref, f32[32,8,128]{2,1,0:T(8,128)} %all_to_all.16.parts_ref, f32[32,8192]{1,0:T(8,128)} %direction_ref.3, f32[32,256]{1,0:T(8,128)} %residual_ref.1, f32[32,256]{1,0:T(8,128)} %iterate_ref.1, ...), custom_call_target="tpu_custom_call" | custom-call | tf_op jit(solution)/shard_map/update/pallas_call | solution.py:283
  (6 shorter events, 0.0 us)
Async XLA Ops:
  2.8 10.0 %collective-permute-start = (bf16[16,8192]{1,0:T(8,128)(2,1)S(1)}, bf16[16,8192]{1,0:T(8,128)(2,1)S(1)}, u32[]{:S(2)}, u32[]{:S(2)}) collective-permute-start(bf16[16,8192]{1,0:T(8,128)(2,1)S(1)} %get-tuple-element.8), channel_id=1, source_target_pairs={{0,1},{1,2},{2,3},{3,4},{4,5},{5,6},{6,7},{8,9},{9,10},{10,11},{11... | collective-permute-start | bytes 786440 | tf_op jit(solution)/shard_map/ppermute | solution.py:238
  7.3 7.7 %collective-permute-start.1 = (bf16[16,8192]{1,0:T(8,128)(2,1)S(1)}, bf16[16,8192]{1,0:T(8,128)(2,1)S(1)}, u32[]{:S(2)}, u32[]{:S(2)}) collective-permute-start(bf16[16,8192]{1,0:T(8,128)(2,1)S(1)} %get-tuple-element.7), channel_id=1, source_target_pairs={{1,0},{2,1},{3,2},{4,3},{5,4},{6,5},{7,6},{9,8},{10,9},{11,10},{12... | collective-permute-start | bytes 786440 | tf_op jit(solution)/shard_map/ppermute | solution.py:239
  15.0 1.2 %copy-start = (f32[32,8192]{1,0:T(8,128)S(1)}, f32[32,8192]{1,0:T(8,128)}, u32[]{:S(2)}) copy-start(f32[32,8192]{1,0:T(8,128)} %direction_ref.3) | copy-start | bytes 3145732
  16.3 3.4 %copy-start.1 = (bf16[64,4,128,128]{3,2,1,0:T(8,128)(2,1)S(1)}, bf16[64,4,128,128]{3,2,1,0:T(8,128)(2,1)}, u32[]{:S(2)}) copy-start(bf16[64,4,128,128]{3,2,1,0:T(8,128)(2,1)} %tiles_hbm.1) | copy-start | bytes 25165828
  19.6 1.2 %copy-start.2 = (bf16[2,32,8192]{2,1,0:T(8,128)(2,1)S(1)}, bf16[2,32,8192]{2,1,0:T(8,128)(2,1)}, u32[]{:S(2)}) copy-start(bf16[2,32,8192]{2,1,0:T(8,128)(2,1)} %members_ref.1) | copy-start | bytes 3145732
  35.7 26.1 %all-to-all-start = ((bf16[32,32,256]{2,1,0:T(8,128)(2,1)}), bf16[32,32,256]{2,1,0:T(8,128)(2,1)S(1)}, u32[]{:S(2)}, u32[]{:S(2)}) async-start(bf16[32,32,256]{2,1,0:T(8,128)(2,1)} %product.1), calls=%async_computation | async-start | bytes 1048576 | tf_op jit(solution)/shard_map/all_to_all | solution.py:260
  61.8 0.8 copy-start.3

commit v2 on v0

v2 whole, which is shorter than its diff:
```python
import functools

import jax
import jax.numpy as jnp
from jax import lax
from jax.experimental import pallas as pl
from jax.experimental.pallas import tpu as pltpu
from jax.sharding import PartitionSpec as P

REACH = 4
HALO = 2 * REACH
EDGE_CHUNKS = 4
TILE_CHUNKS = 8
F32 = jnp.float32
BF16 = jnp.bfloat16
NT = (((1,), (1,)), ((), ()))
VMEM = pl.BlockSpec(memory_space=pltpu.VMEM)
HBM = pl.BlockSpec(memory_space=pltpu.HBM)


def edge_kernel(members_hbm, direction_hbm, low_ref, high_ref, members_ref, direction_ref, sems):
    mem_dev, lev_dev, points = members_ref.shape
    step = points // EDGE_CHUNKS

    def copies(i):
        cols = pl.ds(i * step, step)
        return (
            pltpu.make_async_copy(direction_hbm.at[:, cols], direction_ref.at[:, cols], sems.at[2 * i]),
            pltpu.make_async_copy(members_hbm.at[:, :, cols], members_ref.at[:, :, cols], sems.at[2 * i + 1]),
        )

    for i in range(EDGE_CHUNKS):
        for copy in copies(i):
            copy.start()
    for i in range(EDGE_CHUNKS):
        for copy in copies(i):
            copy.wait()
        cols = slice(i * step, (i + 1) * step)
        low, high = [], []
        for m in range(mem_dev):
            low.append(members_ref[m, : 2 * HALO, cols].astype(F32)[:HALO] * direction_ref[:HALO, cols])
            high.append(members_ref[m, lev_dev - 2 * HALO :, cols].astype(F32)[HALO:] * direction_ref[lev_dev - HALO :, cols])
        low_ref[:, cols] = jnp.concatenate(low, axis=0).astype(BF16)
        high_ref[:, cols] = jnp.concatenate(high, axis=0).astype(BF16)


def split3(value):
    high = value.astype(BF16)
    rest = value - high.astype(F32)
    middle = rest.astype(BF16)
    low = (rest - middle.astype(F32)).astype(BF16)
    return jnp.concatenate([high, middle, low], axis=0)


def level_matrix(band, level_start, levels, lev_dev, mem_dev):
    span = band.shape[0]
    lanes = 128
    row = lax.broadcasted_iota(jnp.int32, (span, lanes), 0)
    col = lax.broadcasted_iota(jnp.int32, (span, lanes), 1)
    dense = jnp.zeros((span, lanes), F32)
    for offset in range(2 * REACH + 1):
        dense = jnp.where(col == row + offset, band[:, offset : offset + 1], dense)
    level = col + (level_start - HALO - REACH)
    dense = jnp.where((level >= 0) & (level < levels), dense, 0.0)
    own, low, high = dense[HALO : HALO + lev_dev], dense[:HALO], dense[HALO + lev_dev :]
    rows = jnp.concatenate([own] * mem_dev, axis=0)
    cols = jnp.concatenate([own] * mem_dev + [low] * mem_dev + [high] * mem_dev, axis=0)
    both = lax.dot_general(rows, cols, NT, precision=lax.Precision.HIGHEST, preferred_element_type=F32)
    i = lax.broadcasted_iota(jnp.int32, both.shape, 0)
    j = lax.broadcasted_iota(jnp.int32, both.shape, 1)
    keep = jnp.zeros(both.shape, jnp.bool_)
    vectors = mem_dev * lev_dev
    for m in range(mem_dev):
        mine = (i >= m * lev_dev) & (i < (m + 1) * lev_dev)
        theirs = (j >= m * lev_dev) & (j < (m + 1) * lev_dev)
        for first in (vectors + m * HALO, vectors + (mem_dev + m) * HALO):
            theirs = theirs | ((j >= first) & (j < first + HALO))
        keep = keep | (mine & theirs)
    return jnp.where(keep, both, 0.0)


def stage_kernel(
    vertical_ref, direction_ref, tiles_hbm, residual_hbm, iterate_hbm,
    tiles_ref, residual_ref, iterate_ref, own_ref, band_ref, padded_ref, sems,
    *, mem_dev,
):
    copies = [
        pltpu.make_async_copy(residual_hbm, residual_ref, sems.at[0]),
        pltpu.make_async_copy(iterate_hbm, iterate_ref, sems.at[1]),
    ]
    part = tiles_ref.shape[0] // TILE_CHUNKS
    for i in range(TILE_CHUNKS):
        rows = pl.ds(i * part, part)
        copies.append(pltpu.make_async_copy(tiles_hbm.at[rows], tiles_ref.at[rows], sems.at[2 + i]))
    for copy in copies:
        copy.start()
    lev_dev, share = own_ref.shape
    levels, width = vertical_ref.shape
    level_start = lax.axis_index("slab") * lev_dev
    own_ref[...] = direction_ref[:, pl.ds(pl.multiple_of(lax.axis_index("member") * share, share), share)]
    padded_ref[...] = jnp.zeros_like(padded_ref)
    padded_ref[HALO : HALO + levels, :width] = vertical_ref[...]
    band = padded_ref[pl.ds(pl.multiple_of(level_start, lev_dev), lev_dev + 2 * HALO), :]
    band_ref[...] = split3(level_matrix(band, level_start, levels, lev_dev, mem_dev))
    for copy in copies:
        copy.wait()


def product_kernel(
    columns_hbm, band_ref, members_ref, direction_ref, below_ref, above_ref, tiles_ref,
    out_ref, columns_ref, smooth_ref, acc_ref, back_ref, sem,
):
    mem_dev, lev_dev, points = members_ref.shape
    blocks, per_row, tile, _ = tiles_ref.shape
    vectors = mem_dev * lev_dev
    fetch = pltpu.make_async_copy(columns_hbm, columns_ref, sem)
    fetch.start()
    band = band_ref[...]
    acc_ref[...] = jnp.zeros_like(acc_ref)

    def vertical_step(g, carry):
        cols = pl.ds(pl.multiple_of(g * 2 * tile, 2 * tile), 2 * tile)
        field = direction_ref[:, cols]
        mixed = [(members_ref[m, :, cols].astype(F32) * field).astype(BF16) for m in range(mem_dev)]
        stacked = jnp.concatenate(mixed + [below_ref[:, cols], above_ref[:, cols]], axis=0)
        three = jnp.dot(band, stacked, preferred_element_type=F32)
        total = (three[2 * vectors :] + three[vectors : 2 * vectors]) + three[:vectors]
        total = total.astype(BF16)
        smooth_ref[2 * g] = total[:, :tile]
        smooth_ref[2 * g + 1] = total[:, tile:]
        return carry

    lax.fori_loop(0, blocks // 2, vertical_step, 0, unroll=8)
    fetch.wait()

    def adjoint_step(r, carry):
        left = smooth_ref[r]
        where = [columns_ref[r, j] for j in range(per_row)]
        right = jnp.concatenate([tiles_ref[r, j] for j in range(per_row)], axis=1)
        spread = jnp.dot(left, right, preferred_element_type=F32)
        new = [acc_ref[where[j]] + spread[:, j * tile : (j + 1) * tile] for j in range(per_row)]
        for j in range(per_row):
            acc_ref[where[j]] = new[j]
        return carry

    lax.fori_loop(0, blocks, adjoint_step, 0, unroll=4)
    back_ref[...] = acc_ref[...].astype(BF16)

    def forward_row(r):
        left = jnp.concatenate([back_ref[columns_ref[r, j]] for j in range(per_row)], axis=1)
        right = jnp.concatenate([tiles_ref[r, j] for j in range(per_row)], axis=1)
        field = lax.dot_general(left, right, NT, preferred_element_type=F32)
        cols = pl.ds(pl.multiple_of(r * tile, tile), tile)
        total = members_ref[0, :, cols].astype(F32) * field[:lev_dev]
        for m in range(1, mem_dev):
            total = total + members_ref[m, :, cols].astype(F32) * field[m * lev_dev : (m + 1) * lev_dev]
        return total

    wide = out_ref.shape[2] // tile

    def forward_step(g, carry):
        for k in range(wide):
            out_ref[g, :, k * tile : (k + 1) * tile] = forward_row(g * wide + k).astype(out_ref.dtype)
        return carry

    lax.fori_loop(0, blocks // wide, forward_step, 0, unroll=8)


def full_sum(value):
    return jnp.sum(jnp.sum(value, axis=0, keepdims=True), axis=1, keepdims=True)


def image_kernel(parts_ref, own_ref, residual_ref, image_ref, sums_ref, *, scale):
    total = parts_ref[0].astype(F32)
    for i in range(1, parts_ref.shape[0]):
        total = total + parts_ref[i].astype(F32)
    own = own_ref[...]
    residual = residual_ref[...]
    image = own + total / scale
    image_ref[...] = image
    rr = full_sum(residual * residual)
    di = full_sum(own * image)
    ii = full_sum(image * image)
    ri = full_sum(residual * image)
    guess = jnp.where(ii > 0.0, ri / jnp.where(ii > 0.0, ii, 1.0), 0.0)
    left = residual - guess * image
    ll = full_sum(left * left)
    li = full_sum(left * image)
    lane = lax.broadcasted_iota(jnp.int32, (1, sums_ref.shape[1]), 1)
    row = jnp.zeros(lane.shape, F32)
    for k, value in enumerate((rr, di, ll, li, ii, guess)):
        row = jnp.where(lane == k, value, row)
    sums_ref[...] = jnp.broadcast_to(row, sums_ref.shape)


def update_kernel(parts_ref, own_ref, residual_ref, iterate_ref, image_ref, x_ref, r_ref, d_ref):
    parts = parts_ref[...]
    sums = jnp.sum(parts, axis=0, keepdims=True)
    norm_old = sums[:, 0:1]
    alpha = norm_old / sums[:, 1:2]
    ll, li, ii, guess = (parts[:, k : k + 1] for k in range(2, 6))
    shift = guess - alpha
    norm_new = jnp.sum(ll + shift * (2.0 * li + shift * ii), axis=0, keepdims=True)
    own = own_ref[...]
    residual_new = residual_ref[...] - alpha * image_ref[...]
    x_ref[...] = iterate_ref[...] + alpha * own
    r_ref[...] = residual_new
    d_ref[...] = residual_new + (norm_new / norm_old) * own


def on_device(members, direction, residual, iterate, tiles, columns, vertical):
    mem_dev, lev_dev, points = members.shape
    blocks, per_row, tile = tiles.shape[:3]
    vectors = mem_dev * lev_dev
    groups, slabs = lax.axis_size("member"), lax.axis_size("slab")
    share = points // groups
    member_count = mem_dev * groups
    levels, width = vertical.shape
    square = (lev_dev, share)
    edge = (mem_dev * HALO, points)

    far = functools.partial(pltpu.with_memory_space_constraint, memory_space=pltpu.HBM)
    low, high, members_near, direction_near = pl.pallas_call(
        edge_kernel,
        out_shape=(
            pltpu.VMEM(edge, BF16), pltpu.VMEM(edge, BF16),
            pltpu.VMEM(members.shape, BF16), pltpu.VMEM(direction.shape, F32),
        ),
        in_specs=[HBM, HBM],
        out_specs=(VMEM,) * 4,
        scratch_shapes=[pltpu.SemaphoreType.DMA((2 * EDGE_CHUNKS,))],
        compiler_params=pltpu.CompilerParams(vmem_limit_bytes=32 * 2**20),
        name="edge",
    )(far(members), far(direction))
    below = lax.ppermute(high, "slab", [(i, (i + 1) % slabs) for i in range(slabs)])
    above = lax.ppermute(low, "slab", [((i + 1) % slabs, i) for i in range(slabs)])

    tiles_near, residual_near, iterate_near, own, band = pl.pallas_call(
        functools.partial(stage_kernel, mem_dev=mem_dev),
        out_shape=(
            pltpu.VMEM(tiles.shape, BF16), pltpu.VMEM(square, F32), pltpu.VMEM(square, F32), pltpu.VMEM(square, F32),
            pltpu.VMEM((3 * vectors, vectors + 2 * mem_dev * HALO), BF16),
        ),
        in_specs=[VMEM, VMEM, HBM, HBM, HBM],
        out_specs=(VMEM,) * 5,
        scratch_shapes=[
            pltpu.VMEM((levels + 2 * HALO, 128), F32),
            pltpu.SemaphoreType.DMA((2 + TILE_CHUNKS,)),
        ],
        compiler_params=pltpu.CompilerParams(vmem_limit_bytes=32 * 2**20),
        cost_estimate=pl.CostEstimate(flops=0, bytes_accessed=2 * tiles.size * 2, transcendentals=0),
        name="stage",
    )(vertical, direction_near, far(tiles), far(residual), far(iterate))

    partial_value = pl.pallas_call(
        product_kernel,
        out_shape=pltpu.VMEM((groups, lev_dev, share), BF16),
        in_specs=[HBM] + [VMEM] * 6,
        out_specs=VMEM,
        scratch_shapes=[
            pltpu.SMEM((blocks, per_row), jnp.int32),
            pltpu.VMEM((blocks, vectors, tile), BF16),
            pltpu.VMEM((blocks, vectors, tile), F32),
            pltpu.VMEM((blocks, vectors, tile), BF16),
            pltpu.SemaphoreType.DMA,
        ],
        compiler_params=pltpu.CompilerParams(vmem_limit_bytes=32 * 2**20),
        name="product",
    )(far(columns), band, members_near, direction_near, below, above, tiles_near)

    parts = lax.all_to_all(partial_value, "member", 0, 0, tiled=True)
    devices = groups * slabs
    image, sums = pl.pallas_call(
        functools.partial(image_kernel, scale=float(member_count - 1)),
        out_shape=(pltpu.VMEM(square, F32), pltpu.VMEM((devices, 128), F32)),
        in_specs=[VMEM] * 3,
        out_specs=(VMEM,) * 2,
        name="image",
    )(parts, own, residual_near)

    spread = lax.all_to_all(sums.reshape(devices, 1, 128), ("member", "slab"), 0, 0, tiled=True)
    field = jax.ShapeDtypeStruct(square, F32)
    return pl.pallas_call(
        update_kernel,
        out_shape=(field, field, field),
        in_specs=[VMEM] * 5,
        out_specs=(VMEM,) * 3,
        name="update",
    )(spread.reshape(devices, 128), own, residual_near, iterate_near, image)


def solution(mesh):
    placed = (
        P("member", "slab", None),
        P("slab", None),
        P("slab", "member"),
        P("slab", "member"),
        P(),
        P(),
        P(),
    )
    return jax.shard_map(
        on_device,
        mesh=mesh,
        in_specs=placed,
        out_specs=(P("slab", "member"), P("slab", "member"), P("slab", "member")),
        check_vma=False,
    )
```

time: 400 us -> 72.9 us (0.18)
  waiting for transfers between devices: 150 us -> 0.01 us
  blocking collectives: 152 us -> 49 us
  other arithmetic: 41.7 us -> 0 us
  Pallas kernels: 0 us -> 17.3 us
  between operations: 17 us -> 0.72 us
  matrix products: 13 us -> 0 us
  starting transfers between devices: 13.6 us -> 3.27 us
  local copies, waits for them, and re-layouts: 11.2 us -> 2.23 us
    psum x2 -> x0, blocking collectives: 152 us -> none  [the longest x1 79 us: on_device(): lax.psum((jnp.sum(residual * residual), jnp.sum(own_direction * image)),...]
    psum x1 -> x0, waiting for transfers between devices: 147 us -> none  [on_device(): summed = lax.psum(partial_value, 'member')]
    all_to_all x0 -> x2, blocking collectives: none -> 49 us  [the longest x1 25.1 us: on_device(): parts = lax.all_to_all(partial_value, 'member', 0, 0, tiled=True)]
    scatter-add x4 -> x0, other arithmetic: 28 us -> none  [on_device(): back = back.at[:, columns[:, column_slot], :].add(spread[column_slot])]
    pallas_call x0 -> x5, Pallas kernels: none -> 17.3 us  [the longest x1 8.75 us: on_device(): pl.pallas_call(product_kernel, out_shape=pltpu.VMEM((groups, lev_dev, sha...]
    dot_general x2 -> x0, matrix products: 13 us -> none  [the longest x1 7.61 us: on_device(): jnp.einsum('vrjb,rjab->vra', picked, tiles, preferred_element_type=jnp.fl...]
    ppermute x4 -> x2, starting transfers between devices: 13.5 us -> 3.27 us  [the longest x1 2.61 us: on_device(): lax.ppermute(high, 'slab', [(i, (i + 1) % slabs) for i in range(slabs)])]
    reduce_sum x4 -> x0, other arithmetic: 7.52 us -> none  [the longest x1 4.13 us: on_device(): partial_value = jnp.sum(wide_members * smoothed, axis=0)]
  transfers between devices with their start and end apart: 5 -> 2, of which waited for: 4 -> 0; matrix products, arithmetic and copies ran while one was open for 0% -> 3% of each run, Pallas kernels for 0% -> 5%
where the time goes in v2:
time: 72.9 us; the launch traced here: 72.6 us
  blocking collectives  49 us (67%)
  Pallas kernels  17.3 us (24%)
  starting transfers between devices  3.27 us (4%)
  local copies, waits for them, and re-layouts  2.23 us (3%)
    all_to_all x1, blocking collectives, on_device(): parts = lax.all_to_all(partial_value, 'member', 0, 0, tiled=True)  25.1 us
    all_to_all x1, blocking collectives, on_device(): lax.all_to_all(sums.reshape(devices, 1, 128), ('member', 'slab'), 0, 0, t...  23.9 us
    pallas_call x1, Pallas kernels, on_device(): pl.pallas_call(product_kernel, out_shape=pltpu.VMEM((groups, lev_dev, sha...  8.75 us
    pallas_call x1, Pallas kernels, on_device(): pl.pallas_call(functools.partial(stage_kernel, mem_dev=mem_dev), out_shap...  3.54 us
    ppermute x1, starting transfers between devices, on_device(): lax.ppermute(high, 'slab', [(i, (i + 1) % slabs) for i in range(slabs)])  2.61 us
    unnamed x10, local copies, waits for them, and re-layouts  2.23 us
    pallas_call x1, Pallas kernels, on_device(): pl.pallas_call(update_kernel, out_shape=(field, field, field), in_specs=[...  2.11 us
    pallas_call x1, Pallas kernels, on_device(): pl.pallas_call(edge_kernel, out_shape=(pltpu.VMEM(edge, BF16), pltpu.VMEM...  1.6 us
  transfers between devices with their start and end apart: 2, of which 0 were waited for; matrix products, arithmetic and copies ran while one was open for 3% of the time, Pallas kernels for 5%

profile of v2, /device:TPU:1, one launch (start us, length us, event | category | flops | bytes accessed | tf_op | source)
XLA Modules:
  0.0 72.6 jit_solution(5834792315301185265)
XLA Ops:
  0.6 1.6 %edge.1 = (bf16[16,8192]{1,0:T(8,128)(2,1)S(1)}, bf16[16,8192]{1,0:T(8,128)(2,1)S(1)}, bf16[2,32,8192]{2,1,0:T(8,128)(2,1)S(1)}, f32[32,8192]{1,0:T(8,128)S(1)}) custom-call(bf16[2,32,8192]{2,1,0:T(8,128)(2,1)} %members_hbm.1, f32[32,8192]{1,0:T(8,128)} %direction_hbm.1), custom_call_target="tpu_custom_call" | custom-call | tf_op jit(solution)/shard_map/edge/pallas_call | solution.py:223
  2.2 2.6 %collective-permute-start = (bf16[16,8192]{1,0:T(8,128)(2,1)S(1)}, bf16[16,8192]{1,0:T(8,128)(2,1)S(1)}, u32[]{:S(2)}, u32[]{:S(2)}) collective-permute-start(bf16[16,8192]{1,0:T(8,128)(2,1)S(1)} %get-tuple-element.17), channel_id=1, source_target_pairs={{0,1},{1,2},{2,3},{3,4},{4,5},{5,6},{6,7},{7,0},{8,9},{9,10},{10,1... | collective-permute-start | bytes 786440 | tf_op jit(solution)/shard_map/ppermute | solution.py:235
  4.8 0.7 collective-permute-start.1
  5.5 1.4 %copy.13.columns_hbm = s32[64,4]{1,0:T(8,128)} copy(s32[64,4]{0,1:T(4,128)} %param.12) | data formatting | bytes 2048 | tf_op args[5]
  6.9 0.8 %copy.12.vertical_ref = f32[256,9]{1,0:T(8,128)S(1)} copy(f32[256,9]{0,1:T(8,128)} %param.13) | data formatting | bytes 18432 | tf_op args[6]
  7.7 3.5 %stage.1 = (bf16[64,4,128,128]{3,2,1,0:T(8,128)(2,1)S(1)}, f32[32,256]{1,0:T(8,128)S(1)}, f32[32,256]{1,0:T(8,128)S(1)}, f32[32,256]{1,0:T(8,128)S(1)}, bf16[192,96]{1,0:T(8,128)(2,1)S(1)}) custom-call(f32[256,9]{1,0:T(8,128)S(1)} %copy.12.vertical_ref, f32[32,8192]{1,0:T(8,128)S(1)} %get-tuple-element.14.direction_ref, bf16[64,4,128,128]{3,2,1,0:T(8,128)(2,1)} %tiles_hbm.1, ...), custom_call_target="tpu_custom_call" | custom-call | bytes 16777216 | tf_op jit(solution)/shard_map/stage/pallas_call | solution.py:238
  11.3 0.0 copy-start
  11.3 0.0 copy-start.1
  11.3 0.0 copy-start.2
  11.3 0.0 collective-permute-done.below_ref
  11.3 0.0 collective-permute-done.1.above_ref
  11.3 8.7 %product.1 = bf16[32,32,256]{2,1,0:T(8,128)(2,1)S(1)} custom-call(s32[64,4]{1,0:T(8,128)} %copy.13.columns_hbm, bf16[192,96]{1,0:T(8,128)(2,1)S(1)} %get-tuple-element.15.band_ref, bf16[2,32,8192]{2,1,0:T(8,128)(2,1)S(1)} %get-tuple-element.16.members_ref, f32[32,8192]{1,0:T(8,128)S(1)} %get-tuple-element.14.direction_ref, ...), custom_call_target="tpu_custom_call" | custom-call | tf_op jit(solution)/shard_map/product/pallas_call | solution.py:255
  20.1 25.1 %all_to_all.10.parts_ref = bf16[32,32,256]{2,1,0:T(8,128)(2,1)} all-to-all(bf16[32,32,256]{2,1,0:T(8,128)(2,1)S(1)} %product.1), channel_id=1, replica_groups=mesh['member'=32,'slab'=8] {'member'}, dimensions={0} | all-to-all | bytes 1048576 | tf_op jit(solution)/shard_map/all_to_all | solution.py:271
  45.2 0.0 copy-done
  45.2 0.0 copy-done.1
  45.2 0.0 copy-done.2
  45.2 1.3 %image.1 = (f32[32,256]{1,0:T(8,128)S(1)}, f32[256,128]{1,0:T(8,128)S(1)}) custom-call(bf16[32,32,256]{2,1,0:T(8,128)(2,1)} %all_to_all.10.parts_ref, f32[32,256]{1,0:T(8,128)} %copy-done.1, f32[32,256]{1,0:T(8,128)} %copy-done), custom_call_target="tpu_custom_call" | custom-call | tf_op jit(solution)/shard_map/image/pallas_call | solution.py:273
  46.6 0.0 copy-start.3
  46.6 23.9 %all_to_all.11 = f32[256,1,128]{2,1,0:T(1,128)} all-to-all(f32[256,1,128]{2,1,0:T(1,128)S(1)} %bitcast.4), channel_id=1, replica_groups=mesh['member'=32,'slab'=8] {'member','slab'}, dimensions={0} | all-to-all | bytes 262144 | tf_op jit(solution)/shard_map/all_to_all | solution.py:281
  70.5 0.0 copy-done.3
  70.5 2.1 %update.1 = (f32[32,256]{1,0:T(8,128)}, f32[32,256]{1,0:T(8,128)}, f32[32,256]{1,0:T(8,128)}) custom-call(f32[256,128]{1,0:T(8,128)} %bitcast.5, f32[32,256]{1,0:T(8,128)} %copy-done.1, f32[32,256]{1,0:T(8,128)} %copy-done, f32[32,256]{1,0:T(8,128)} %copy-done.2, f32[32,256]{1,0:T(8,128)} %copy-done.3), custom_call_target="tpu_custom_call" | custom-call | tf_op jit(solution)/shard_map/update/pallas_call | solution.py:283
Async XLA Ops:
  2.2 9.1 %collective-permute-start = (bf16[16,8192]{1,0:T(8,128)(2,1)S(1)}, bf16[16,8192]{1,0:T(8,128)(2,1)S(1)}, u32[]{:S(2)}, u32[]{:S(2)}) collective-permute-start(bf16[16,8192]{1,0:T(8,128)(2,1)S(1)} %get-tuple-element.17), channel_id=1, source_target_pairs={{0,1},{1,2},{2,3},{3,4},{4,5},{5,6},{6,7},{7,0},{8,9},{9,10},{10,1... | collective-permute-start | bytes 786440 | tf_op jit(solution)/shard_map/ppermute | solution.py:235
  4.8 6.5 %collective-permute-start.1 = (bf16[16,8192]{1,0:T(8,128)(2,1)S(1)}, bf16[16,8192]{1,0:T(8,128)(2,1)S(1)}, u32[]{:S(2)}, u32[]{:S(2)}) collective-permute-start(bf16[16,8192]{1,0:T(8,128)(2,1)S(1)} %get-tuple-element.18), channel_id=1, source_target_pairs={{1,0},{2,1},{3,2},{4,3},{5,4},{6,5},{7,6},{0,7},{9,8},{10,9},{11,1... | collective-permute-start | bytes 786440 | tf_op jit(solution)/shard_map/ppermute | solution.py:236
  11.3 33.9 %copy-start = (f32[32,256]{1,0:T(8,128)}, f32[32,256]{1,0:T(8,128)S(1)}, u32[]{:S(2)}) copy-start(f32[32,256]{1,0:T(8,128)S(1)} %get-tuple-element.21.residual_ref) | copy-start | bytes 98308
  11.3 33.9 %copy-start.1 = (f32[32,256]{1,0:T(8,128)}, f32[32,256]{1,0:T(8,128)S(1)}, u32[]{:S(2)}) copy-start(f32[32,256]{1,0:T(8,128)S(1)} %get-tuple-element.20.own_ref) | copy-start | bytes 98308
  11.3 33.9 %copy-start.2 = (f32[32,256]{1,0:T(8,128)}, f32[32,256]{1,0:T(8,128)S(1)}, u32[]{:S(2)}) copy-start(f32[32,256]{1,0:T(8,128)S(1)} %get-tuple-element.23.iterate_ref) | copy-start | bytes 98308
  46.6 23.9 %copy-start.3 = (f32[32,256]{1,0:T(8,128)}, f32[32,256]{1,0:T(8,128)S(1)}, u32[]{:S(2)}) copy-start(f32[32,256]{1,0:T(8,128)S(1)} %get-tuple-element.24.image_ref) | copy-start | bytes 98308

commit v3 on v2

--- a/solution.py
+++ b/solution.py
@@ -11,6 +11,7 @@
 HALO = 2 * REACH
 EDGE_CHUNKS = 4
 TILE_CHUNKS = 8
+LANES = 128
 F32 = jnp.float32
 BF16 = jnp.bfloat16
 NT = (((1,), (1,)), ((), ()))
@@ -18,15 +19,17 @@
 HBM = pl.BlockSpec(memory_space=pltpu.HBM)
 
 
-def edge_kernel(members_hbm, direction_hbm, low_ref, high_ref, members_ref, direction_ref, sems):
+def edge_kernel(members_hbm, direction_hbm, low_ref, high_ref, members_ref, rim_ref, sems):
     mem_dev, lev_dev, points = members_ref.shape
     step = points // EDGE_CHUNKS
 
     def copies(i):
         cols = pl.ds(i * step, step)
+        last = pl.ds(lev_dev - HALO, HALO)
         return (
-            pltpu.make_async_copy(direction_hbm.at[:, cols], direction_ref.at[:, cols], sems.at[2 * i]),
-            pltpu.make_async_copy(members_hbm.at[:, :, cols], members_ref.at[:, :, cols], sems.at[2 * i + 1]),
+            pltpu.make_async_copy(direction_hbm.at[pl.ds(0, HALO), cols], rim_ref.at[0, :, cols], sems.at[3 * i]),
+            pltpu.make_async_copy(direction_hbm.at[last, cols], rim_ref.at[1, :, cols], sems.at[3 * i + 1]),
+            pltpu.make_async_copy(members_hbm.at[:, :, cols], members_ref.at[:, :, cols], sems.at[3 * i + 2]),
         )
 
     for i in range(EDGE_CHUNKS):
@@ -38,8 +41,8 @@
         cols = slice(i * step, (i + 1) * step)
         low, high = [], []
         for m in range(mem_dev):
-            low.append(members_ref[m, : 2 * HALO, cols].astype(F32)[:HALO] * direction_ref[:HALO, cols])
-            high.append(members_ref[m, lev_dev - 2 * HALO :, cols].astype(F32)[HALO:] * direction_ref[lev_dev - HALO :, cols])
+            low.append(members_ref[m, : 2 * HALO, cols].astype(F32)[:HALO] * rim_ref[0, :, cols])
+            high.append(members_ref[m, lev_dev - 2 * HALO :, cols].astype(F32)[HALO:] * rim_ref[1, :, cols])
         low_ref[:, cols] = jnp.concatenate(low, axis=0).astype(BF16)
         high_ref[:, cols] = jnp.concatenate(high, axis=0).astype(BF16)
 
@@ -80,28 +83,32 @@
 
 
 def stage_kernel(
-    vertical_ref, direction_ref, tiles_hbm, residual_hbm, iterate_hbm,
-    tiles_ref, residual_ref, iterate_ref, own_ref, band_ref, padded_ref, sems,
+    vertical_ref, direction_hbm, tiles_hbm, residual_hbm, iterate_hbm,
+    tiles_ref, direction_ref, residual_ref, iterate_ref, own_ref, band_ref, padded_ref, sems,
     *, mem_dev,
 ):
+    lev_dev, share = own_ref.shape
+    mine = pl.ds(pl.multiple_of(lax.axis_index("member") * share, share), share)
     copies = [
-        pltpu.make_async_copy(residual_hbm, residual_ref, sems.at[0]),
-        pltpu.make_async_copy(iterate_hbm, iterate_ref, sems.at[1]),
+        pltpu.make_async_copy(direction_hbm, direction_ref, sems.at[0]),
+        pltpu.make_async_copy(direction_hbm.at[:, mine], own_ref, sems.at[1]),
+        pltpu.make_async_copy(residual_hbm, residual_ref, sems.at[2]),
+        pltpu.make_async_copy(iterate_hbm, iterate_ref, sems.at[3]),
     ]
     part = tiles_ref.shape[0] // TILE_CHUNKS
     for i in range(TILE_CHUNKS):
         rows = pl.ds(i * part, part)
-        copies.append(pltpu.make_async_copy(tiles_hbm.at[rows], tiles_ref.at[rows], sems.at[2 + i]))
+        copies.append(pltpu.make_async_copy(tiles_hbm.at[rows], tiles_ref.at[rows], sems.at[4 + i]))
     for copy in copies:
         copy.start()
-    lev_dev, share = own_ref.shape
-    levels, width = vertical_ref.shape
+    width, levels = vertical_ref.shape
     level_start = lax.axis_index("slab") * lev_dev
-    own_ref[...] = direction_ref[:, pl.ds(pl.multiple_of(lax.axis_index("member") * share, share), share)]
     padded_ref[...] = jnp.zeros_like(padded_ref)
-    padded_ref[HALO : HALO + levels, :width] = vertical_ref[...]
-    band = padded_ref[pl.ds(pl.multiple_of(level_start, lev_dev), lev_dev + 2 * HALO), :]
-    band_ref[...] = split3(level_matrix(band, level_start, levels, lev_dev, mem_dev))
+    padded_ref[:width, LANES : LANES + levels] = vertical_ref[...]
+    total = padded_ref.shape[1]
+    turned = pltpu.roll(padded_ref[...], total - (LANES - HALO + level_start), 1)[:, :LANES]
+    band = jnp.concatenate([turned, jnp.zeros((LANES - turned.shape[0], LANES), F32)], axis=0).T
+    band_ref[...] = split3(level_matrix(band[: lev_dev + 2 * HALO], level_start, levels, lev_dev, mem_dev))
     for copy in copies:
         copy.wait()
 
@@ -116,7 +123,6 @@
     fetch = pltpu.make_async_copy(columns_hbm, columns_ref, sem)
     fetch.start()
     band = band_ref[...]
-    acc_ref[...] = jnp.zeros_like(acc_ref)
 
     def vertical_step(g, carry):
         cols = pl.ds(pl.multiple_of(g * 2 * tile, 2 * tile), 2 * tile)
@@ -128,14 +134,16 @@
         total = total.astype(BF16)
         smooth_ref[2 * g] = total[:, :tile]
         smooth_ref[2 * g + 1] = total[:, tile:]
+        for k in range(2):
+            acc_ref[2 * g + k] = jnp.zeros((vectors, tile), F32)
         return carry
 
-    lax.fori_loop(0, blocks // 2, vertical_step, 0, unroll=8)
+    lax.fori_loop(0, blocks // 2, vertical_step, 0, unroll=16)
     fetch.wait()
 
     def adjoint_step(r, carry):
         left = smooth_ref[r]
-        where = [columns_ref[r, j] for j in range(per_row)]
+        where = [columns_ref[j, r] for j in range(per_row)]
         right = jnp.concatenate([tiles_ref[r, j] for j in range(per_row)], axis=1)
         spread = jnp.dot(left, right, preferred_element_type=F32)
         new = [acc_ref[where[j]] + spread[:, j * tile : (j + 1) * tile] for j in range(per_row)]
@@ -143,11 +151,11 @@
             acc_ref[where[j]] = new[j]
         return carry
 
-    lax.fori_loop(0, blocks, adjoint_step, 0, unroll=4)
+    lax.fori_loop(0, blocks, adjoint_step, 0, unroll=16)
     back_ref[...] = acc_ref[...].astype(BF16)
 
     def forward_row(r):
-        left = jnp.concatenate([back_ref[columns_ref[r, j]] for j in range(per_row)], axis=1)
+        left = jnp.concatenate([back_ref[columns_ref[j, r]] for j in range(per_row)], axis=1)
         right = jnp.concatenate([tiles_ref[r, j] for j in range(per_row)], axis=1)
         field = lax.dot_general(left, right, NT, preferred_element_type=F32)
         cols = pl.ds(pl.multiple_of(r * tile, tile), tile)
@@ -163,7 +171,7 @@
             out_ref[g, :, k * tile : (k + 1) * tile] = forward_row(g * wide + k).astype(out_ref.dtype)
         return carry
 
-    lax.fori_loop(0, blocks // wide, forward_step, 0, unroll=8)
+    lax.fori_loop(0, blocks // wide, forward_step, 0, unroll=32)
 
 
 def full_sum(value):
@@ -220,37 +228,37 @@
     edge = (mem_dev * HALO, points)
 
     far = functools.partial(pltpu.with_memory_space_constraint, memory_space=pltpu.HBM)
-    low, high, members_near, direction_near = pl.pallas_call(
+    near = functools.partial(pltpu.with_memory_space_constraint, memory_space=pltpu.VMEM)
+    limit = pltpu.CompilerParams(vmem_limit_bytes=32 * 2**20)
+    low, high, members_near = pl.pallas_call(
         edge_kernel,
-        out_shape=(
-            pltpu.VMEM(edge, BF16), pltpu.VMEM(edge, BF16),
-            pltpu.VMEM(members.shape, BF16), pltpu.VMEM(direction.shape, F32),
-        ),
+        out_shape=(pltpu.VMEM(edge, BF16), pltpu.VMEM(edge, BF16), pltpu.VMEM(members.shape, BF16)),
         in_specs=[HBM, HBM],
-        out_specs=(VMEM,) * 4,
-        scratch_shapes=[pltpu.SemaphoreType.DMA((2 * EDGE_CHUNKS,))],
-        compiler_params=pltpu.CompilerParams(vmem_limit_bytes=32 * 2**20),
+        out_specs=(VMEM,) * 3,
+        scratch_shapes=[pltpu.VMEM((2, HALO, points), F32), pltpu.SemaphoreType.DMA((3 * EDGE_CHUNKS,))],
+        compiler_params=limit,
         name="edge",
     )(far(members), far(direction))
     below = lax.ppermute(high, "slab", [(i, (i + 1) % slabs) for i in range(slabs)])
     above = lax.ppermute(low, "slab", [((i + 1) % slabs, i) for i in range(slabs)])
 
-    tiles_near, residual_near, iterate_near, own, band = pl.pallas_call(
+    tiles_near, direction_near, residual_near, iterate_near, own, band = pl.pallas_call(
         functools.partial(stage_kernel, mem_dev=mem_dev),
         out_shape=(
-            pltpu.VMEM(tiles.shape, BF16), pltpu.VMEM(square, F32), pltpu.VMEM(square, F32), pltpu.VMEM(square, F32),
+            pltpu.VMEM(tiles.shape, BF16), pltpu.VMEM(direction.shape, F32),
+            pltpu.VMEM(square, F32), pltpu.VMEM(square, F32), pltpu.VMEM(square, F32),
             pltpu.VMEM((3 * vectors, vectors + 2 * mem_dev * HALO), BF16),
         ),
-        in_specs=[VMEM, VMEM, HBM, HBM, HBM],
-        out_specs=(VMEM,) * 5,
+        in_specs=[VMEM] + [HBM] * 4,
+        out_specs=(VMEM,) * 6,
         scratch_shapes=[
-            pltpu.VMEM((levels + 2 * HALO, 128), F32),
-            pltpu.SemaphoreType.DMA((2 + TILE_CHUNKS,)),
+            pltpu.VMEM((-(-width // 8) * 8, levels + 2 * LANES), F32),
+            pltpu.SemaphoreType.DMA((4 + TILE_CHUNKS,)),
         ],
-        compiler_params=pltpu.CompilerParams(vmem_limit_bytes=32 * 2**20),
+        compiler_params=limit,
         cost_estimate=pl.CostEstimate(flops=0, bytes_accessed=2 * tiles.size * 2, transcendentals=0),
         name="stage",
-    )(vertical, direction_near, far(tiles), far(residual), far(iterate))
+    )(vertical.T, far(direction), far(tiles), far(residual), far(iterate))
 
     partial_value = pl.pallas_call(
         product_kernel,
@@ -258,15 +266,15 @@
         in_specs=[HBM] + [VMEM] * 6,
         out_specs=VMEM,
         scratch_shapes=[
-            pltpu.SMEM((blocks, per_row), jnp.int32),
+            pltpu.SMEM((per_row, blocks), jnp.int32),
             pltpu.VMEM((blocks, vectors, tile), BF16),
             pltpu.VMEM((blocks, vectors, tile), F32),
             pltpu.VMEM((blocks, vectors, tile), BF16),
             pltpu.SemaphoreType.DMA,
         ],
-        compiler_params=pltpu.CompilerParams(vmem_limit_bytes=32 * 2**20),
+        compiler_params=limit,
         name="product",
-    )(far(columns), band, members_near, direction_near, below, above, tiles_near)
+    )(far(columns.T), band, members_near, direction_near, below, above, tiles_near)
 
     parts = lax.all_to_all(partial_value, "member", 0, 0, tiled=True)
     devices = groups * slabs
@@ -275,8 +283,9 @@
         out_shape=(pltpu.VMEM(square, F32), pltpu.VMEM((devices, 128), F32)),
         in_specs=[VMEM] * 3,
         out_specs=(VMEM,) * 2,
+        compiler_params=limit,
         name="image",
-    )(parts, own, residual_near)
+    )(near(parts), own, residual_near)
 
     spread = lax.all_to_all(sums.reshape(devices, 1, 128), ("member", "slab"), 0, 0, tiled=True)
     field = jax.ShapeDtypeStruct(square, F32)
@@ -285,8 +294,9 @@
         out_shape=(field, field, field),
         in_specs=[VMEM] * 5,
         out_specs=(VMEM,) * 3,
+        compiler_params=limit,
         name="update",
-    )(spread.reshape(devices, 128), own, residual_near, iterate_near, image)
+    )(near(spread.reshape(devices, 128)), own, residual_near, iterate_near, image)
 
 
 def solution(mesh):

time: 72.9 us -> 68.2 us (0.936)
  Pallas kernels: 17.3 us -> 13 us
  local copies, waits for them, and re-layouts: 2.23 us -> 0.72 us
  waiting for transfers between devices: 0.01 us -> 0.82 us
    pallas_call x1, Pallas kernels: 8.75 us -> 6.2 us  [on_device(): pl.pallas_call(product_kernel, out_shape=pltpu.VMEM((groups, lev_dev, sha...]
    all_to_all x1, blocking collectives: 25.1 us -> 26.8 us  [on_device(): parts = lax.all_to_all(partial_value, 'member', 0, 0, tiled=True)]
    unnamed x10 -> x2, local copies, waits for them, and re-layouts: 2.23 us -> 0.72 us
    all_to_all x1, blocking collectives: 23.9 us -> 22.6 us  [on_device(): lax.all_to_all(sums.reshape(devices, 1, 128), ('member', 'slab'), 0, 0, t...]
    pallas_call x1, Pallas kernels: 1.33 us -> 0.26 us  [on_device(): pl.pallas_call(functools.partial(image_kernel, scale=float(member_count -...]
    pallas_call x1, Pallas kernels: 2.11 us -> 1.16 us  [on_device(): pl.pallas_call(update_kernel, out_shape=(field, field, field), in_specs=[...]
    ppermute x1, waiting for transfers between devices: 0.01 us -> 0.81 us  [on_device(): lax.ppermute(low, 'slab', [((i + 1) % slabs, i) for i in range(slabs)])]
  transfers between devices with their start and end apart: 2 -> 2, of which waited for: 0 -> 1; matrix products, arithmetic and copies ran while one was open for 3% -> 0% of each run, Pallas kernels for 5% -> 6%
where the time goes in v3:
time: 68.2 us; the launch traced here: 68 us
  blocking collectives  49.5 us (73%)
  Pallas kernels  13 us (19%)
  starting transfers between devices  3.27 us (5%)
  waiting for transfers between devices  0.82 us (1%)
  local copies, waits for them, and re-layouts  0.72 us (1%)
    all_to_all x1, blocking collectives, on_device(): parts = lax.all_to_all(partial_value, 'member', 0, 0, tiled=True)  26.8 us
    all_to_all x1, blocking collectives, on_device(): lax.all_to_all(sums.reshape(devices, 1, 128), ('member', 'slab'), 0, 0, t...  22.6 us
    pallas_call x1, Pallas kernels, on_device(): pl.pallas_call(product_kernel, out_shape=pltpu.VMEM((groups, lev_dev, sha...  6.2 us
    pallas_call x1, Pallas kernels, on_device(): pl.pallas_call(functools.partial(stage_kernel, mem_dev=mem_dev), out_shap...  3.88 us
    ppermute x1, starting transfers between devices, on_device(): lax.ppermute(high, 'slab', [(i, (i + 1) % slabs) for i in range(slabs)])  2.61 us
    pallas_call x1, Pallas kernels, on_device(): pl.pallas_call(edge_kernel, out_shape=(pltpu.VMEM(edge, BF16), pltpu.VMEM...  1.54 us
  transfers between devices with their start and end apart: 2, of which 1 were waited for; matrix products, arithmetic and copies ran while one was open for 0% of the time, Pallas kernels for 6%

profile of v3, /device:TPU:1, one launch (start us, length us, event | category | flops | bytes accessed | tf_op | source)
XLA Modules:
  0.0 68.0 jit_solution(7922372266856742865)
XLA Ops:
  0.6 1.5 %edge.1 = (bf16[16,8192]{1,0:T(8,128)(2,1)S(1)}, bf16[16,8192]{1,0:T(8,128)(2,1)S(1)}, bf16[2,32,8192]{2,1,0:T(8,128)(2,1)S(1)}) custom-call(bf16[2,32,8192]{2,1,0:T(8,128)(2,1)} %members_hbm.1, f32[32,8192]{1,0:T(8,128)} %direction_hbm.3), custom_call_target="tpu_custom_call" | custom-call | tf_op jit(solution)/shard_map/edge/pallas_call | solution.py:233
  2.2 2.6 %collective-permute-start = (bf16[16,8192]{1,0:T(8,128)(2,1)S(1)}, bf16[16,8192]{1,0:T(8,128)(2,1)S(1)}, u32[]{:S(2)}, u32[]{:S(2)}) collective-permute-start(bf16[16,8192]{1,0:T(8,128)(2,1)S(1)} %get-tuple-element.17), channel_id=1, source_target_pairs={{0,1},{1,2},{2,3},{3,4},{4,5},{5,6},{6,7},{7,0},{8,9},{9,10},{10,1... | collective-permute-start | bytes 786440 | tf_op jit(solution)/shard_map/ppermute | solution.py:242
  4.8 0.7 collective-permute-start.1
  5.5 0.0 copy-start
  5.5 0.7 %copy-done = f32[256,9]{0,1:T(8,128)S(1)} copy-done((f32[256,9]{0,1:T(8,128)S(1)}, f32[256,9]{0,1:T(8,128)}, u32[]{:S(2)}) %copy-start) | copy-done | bytes 9240
  6.2 3.9 %stage.1 = (bf16[64,4,128,128]{3,2,1,0:T(8,128)(2,1)S(1)}, f32[32,8192]{1,0:T(8,128)S(1)}, f32[32,256]{1,0:T(8,128)S(1)}, f32[32,256]{1,0:T(8,128)S(1)}, f32[32,...) custom-call(f32[9,256]{1,0:T(8,128)S(1)} %bitcast.8, f32[32,8192]{1,0:T(8,128)} %direction_hbm.3, ...), custom_call_target="tpu_custom_call" | custom-call | bytes 16777216 | tf_op jit(solution)/shard_map/stage/pallas_call | solution.py:245
  10.1 0.0 collective-permute-done.below_ref
  10.1 0.8 %collective-permute-done.1.above_ref = bf16[16,8192]{1,0:T(8,128)(2,1)S(1)} collective-permute-done((bf16[16,8192]{1,0:T(8,128)(2,1)S(1)}, bf16[16,8192]{1,0:T(8,128)(2,1)S(1)}, u32[]{:S(2)}, u32[]{:S(2)}) %collective-permute-start.1) | collective-permute-done | bytes 262176 | tf_op jit(solution)/shard_map/ppermute | solution.py:243
  10.9 6.2 %product.1 = bf16[32,32,256]{2,1,0:T(8,128)(2,1)S(1)} custom-call(s32[4,64]{1,0:T(4,128)} %bitcast.9, bf16[192,96]{1,0:T(8,128)(2,1)S(1)} %get-tuple-element.14.band_ref, bf16[2,32,8192]{2,1,0:T(8,128)(2,1)S(1)} %get-tuple-element.15.members_ref, f32[32,8192]{1,0:T(8,128)S(1)} %get-tuple-element.16.direction_ref, ...), custom_call_target="tpu_custom_call" | custom-call | tf_op jit(solution)/shard_map/product/pallas_call | solution.py:263
  17.1 26.8 %all_to_all.10.parts_ref = bf16[32,32,256]{2,1,0:T(8,128)(2,1)S(1)} all-to-all(bf16[32,32,256]{2,1,0:T(8,128)(2,1)S(1)} %product.1), channel_id=1, replica_groups=mesh['member'=32,'slab'=8] {'member'}, dimensions={0} | all-to-all | bytes 1048576 | tf_op jit(solution)/shard_map/all_to_all | solution.py:279
  43.9 0.3 image.1
  44.2 22.6 %all_to_all.11 = f32[256,1,128]{2,1,0:T(1,128)S(1)} all-to-all(f32[256,1,128]{2,1,0:T(1,128)S(1)} %bitcast.7), channel_id=1, replica_groups=mesh['member'=32,'slab'=8] {'member','slab'}, dimensions={0} | all-to-all | bytes 262144 | tf_op jit(solution)/shard_map/all_to_all | solution.py:290
  66.8 1.2 %update.1 = (f32[32,256]{1,0:T(8,128)}, f32[32,256]{1,0:T(8,128)}, f32[32,256]{1,0:T(8,128)}) custom-call(f32[256,128]{1,0:T(8,128)S(1)} %bitcast.6, f32[32,256]{1,0:T(8,128)S(1)} %get-tuple-element.20.own_ref, f32[32,256]{1,0:T(8,128)S(1)} %get-tuple-element.21.residual_ref, f32[32,256]{1,0:T(8,128)S(1)} %get-tuple-element.23.iterate_ref, ...), custom_call_target="tpu_custom_call" | custom-call | tf_op jit(solution)/shard_map/update/pallas_call | solution.py:292
Async XLA Ops:
  2.2 7.9 %collective-permute-start = (bf16[16,8192]{1,0:T(8,128)(2,1)S(1)}, bf16[16,8192]{1,0:T(8,128)(2,1)S(1)}, u32[]{:S(2)}, u32[]{:S(2)}) collective-permute-start(bf16[16,8192]{1,0:T(8,128)(2,1)S(1)} %get-tuple-element.17), channel_id=1, source_target_pairs={{0,1},{1,2},{2,3},{3,4},{4,5},{5,6},{6,7},{7,0},{8,9},{9,10},{10,1... | collective-permute-start | bytes 786440 | tf_op jit(solution)/shard_map/ppermute | solution.py:242
  4.8 6.1 %collective-permute-start.1 = (bf16[16,8192]{1,0:T(8,128)(2,1)S(1)}, bf16[16,8192]{1,0:T(8,128)(2,1)S(1)}, u32[]{:S(2)}, u32[]{:S(2)}) collective-permute-start(bf16[16,8192]{1,0:T(8,128)(2,1)S(1)} %get-tuple-element.18), channel_id=1, source_target_pairs={{1,0},{2,1},{3,2},{4,3},{5,4},{6,5},{7,6},{0,7},{9,8},{10,9},{11,1... | collective-permute-start | bytes 786440 | tf_op jit(solution)/shard_map/ppermute | solution.py:243
  5.5 0.7 %copy-start = (f32[256,9]{0,1:T(8,128)S(1)}, f32[256,9]{0,1:T(8,128)}, u32[]{:S(2)}) copy-start(f32[256,9]{0,1:T(8,128)} %param.13) | copy-start | bytes 27652

commit v4 on v3

--- a/solution.py
+++ b/solution.py
@@ -12,6 +12,7 @@
 EDGE_CHUNKS = 4
 TILE_CHUNKS = 8
 LANES = 128
+NEAR = 4
 F32 = jnp.float32
 BF16 = jnp.bfloat16
 NT = (((1,), (1,)), ((), ()))
@@ -113,10 +114,28 @@
         copy.wait()
 
 
+def forward_share(g, wide, columns_ref, tiles_ref, back_ref, members_ref):
+    mem_dev, lev_dev, points = members_ref.shape
+    blocks, per_row, tile, _ = tiles_ref.shape
+    pieces = []
+    for k in range(wide):
+        r = g * wide + k
+        left = jnp.concatenate([back_ref[columns_ref[j, r]] for j in range(per_row)], axis=1)
+        right = jnp.concatenate([tiles_ref[r, j] for j in range(per_row)], axis=1)
+        field = lax.dot_general(left, right, NT, preferred_element_type=F32)
+        cols = pl.ds(pl.multiple_of(r * tile, tile), tile)
+        total = members_ref[0, :, cols].astype(F32) * field[:lev_dev]
+        for m in range(1, mem_dev):
+            total = total + members_ref[m, :, cols].astype(F32) * field[m * lev_dev : (m + 1) * lev_dev]
+        pieces.append(total)
+    return jnp.concatenate(pieces, axis=1)
+
+
 def product_kernel(
     columns_hbm, band_ref, members_ref, direction_ref, below_ref, above_ref, tiles_ref,
-    out_ref, columns_ref, smooth_ref, acc_ref, back_ref, sem,
+    back_ref, *rest,
 ):
+    *send_refs, columns_ref, smooth_ref, acc_ref, sem = rest
     mem_dev, lev_dev, points = members_ref.shape
     blocks, per_row, tile, _ = tiles_ref.shape
     vectors = mem_dev * lev_dev
@@ -153,25 +172,41 @@
 
     lax.fori_loop(0, blocks, adjoint_step, 0, unroll=16)
     back_ref[...] = acc_ref[...].astype(BF16)
-
-    def forward_row(r):
-        left = jnp.concatenate([back_ref[columns_ref[j, r]] for j in range(per_row)], axis=1)
-        right = jnp.concatenate([tiles_ref[r, j] for j in range(per_row)], axis=1)
-        field = lax.dot_general(left, right, NT, preferred_element_type=F32)
-        cols = pl.ds(pl.multiple_of(r * tile, tile), tile)
-        total = members_ref[0, :, cols].astype(F32) * field[:lev_dev]
-        for m in range(1, mem_dev):
-            total = total + members_ref[m, :, cols].astype(F32) * field[m * lev_dev : (m + 1) * lev_dev]
-        return total
-
-    wide = out_ref.shape[2] // tile
-
-    def forward_step(g, carry):
-        for k in range(wide):
-            out_ref[g, :, k * tile : (k + 1) * tile] = forward_row(g * wide + k).astype(out_ref.dtype)
+    far_count, _, share = send_refs[0].shape
+    here = lax.axis_index("member") % NEAR
+    for d in range(1, NEAR):
+        target = (here + d) % NEAR
+        out_ref = send_refs[d - 1]
+
+        def forward_step(z, carry, target=target, out_ref=out_ref):
+            value = forward_share(z * NEAR + target, share // tile, columns_ref, tiles_ref, back_ref, members_ref)
+            out_ref[z] = value.astype(out_ref.dtype)
+            return carry
+
+        lax.fori_loop(0, far_count, forward_step, 0, unroll=8)
+
+
+def own_kernel(columns_hbm, members_ref, tiles_ref, back_ref, out_ref, columns_ref, sem):
+    fetch = pltpu.make_async_copy(columns_hbm, columns_ref, sem)
+    fetch.start()
+    fetch.wait()
+    far_count, _, share = out_ref.shape
+    tile = tiles_ref.shape[3]
+    here = lax.axis_index("member") % NEAR
+
+    def forward_step(z, carry):
+        out_ref[z] = forward_share(z * NEAR + here, share // tile, columns_ref, tiles_ref, back_ref, members_ref)
         return carry
 
-    lax.fori_loop(0, blocks // wide, forward_step, 0, unroll=32)
+    lax.fori_loop(0, far_count, forward_step, 0, unroll=8)
+
+
+def fold_kernel(own_ref, *refs):
+    *arrived, out_ref = refs
+    total = own_ref[...]
+    for ref in arrived:
+        total = total + ref[...].astype(F32)
+    out_ref[...] = total.astype(out_ref.dtype)
 
 
 def full_sum(value):
@@ -260,23 +295,49 @@
         name="stage",
     )(vertical.T, far(direction), far(tiles), far(residual), far(iterate))
 
-    partial_value = pl.pallas_call(
+    far_count = groups // NEAR
+    piece = (far_count, lev_dev, share)
+    columns_far = far(columns.T)
+    columns_scratch = [pltpu.SMEM((per_row, blocks), jnp.int32)]
+    back, *sent = pl.pallas_call(
         product_kernel,
-        out_shape=pltpu.VMEM((groups, lev_dev, share), BF16),
+        out_shape=(pltpu.VMEM((blocks, vectors, tile), BF16),) + (pltpu.VMEM(piece, BF16),) * (NEAR - 1),
         in_specs=[HBM] + [VMEM] * 6,
-        out_specs=VMEM,
-        scratch_shapes=[
-            pltpu.SMEM((per_row, blocks), jnp.int32),
+        out_specs=(VMEM,) * NEAR,
+        scratch_shapes=columns_scratch + [
             pltpu.VMEM((blocks, vectors, tile), BF16),
             pltpu.VMEM((blocks, vectors, tile), F32),
-            pltpu.VMEM((blocks, vectors, tile), BF16),
             pltpu.SemaphoreType.DMA,
         ],
         compiler_params=limit,
         name="product",
-    )(far(columns.T), band, members_near, direction_near, below, above, tiles_near)
-
-    parts = lax.all_to_all(partial_value, "member", 0, 0, tiled=True)
+    )(columns_far, band, members_near, direction_near, below, above, tiles_near)
+    arrived = [
+        lax.ppermute(
+            sent[d - 1], "member", [(i, i // NEAR * NEAR + (i + d) % NEAR) for i in range(groups)]
+        )
+        for d in range(1, NEAR)
+    ]
+    own_part = pl.pallas_call(
+        own_kernel,
+        out_shape=pltpu.VMEM(piece, F32),
+        in_specs=[HBM] + [VMEM] * 3,
+        out_specs=VMEM,
+        scratch_shapes=columns_scratch + [pltpu.SemaphoreType.DMA],
+        compiler_params=limit,
+        cost_estimate=pl.CostEstimate(flops=vectors * points * per_row * tile // 2, bytes_accessed=tiles.size // 2, transcendentals=0),
+        name="own",
+    )(columns_far, members_near, tiles_near, back)
+    folded = pl.pallas_call(
+        fold_kernel,
+        out_shape=pltpu.VMEM(piece, BF16),
+        in_specs=[VMEM] * NEAR,
+        out_specs=VMEM,
+        compiler_params=limit,
+        name="fold",
+    )(near(own_part), *(near(x) for x in arrived))
+    columns_of = [[y + NEAR * z for z in range(far_count)] for y in range(NEAR)]
+    parts = lax.all_to_all(folded, "member", 0, 0, axis_index_groups=columns_of, tiled=True)
     devices = groups * slabs
     image, sums = pl.pallas_call(
         functools.partial(image_kernel, scale=float(member_count - 1)),

time: 68.2 us -> 66.3 us (0.972)
  blocking collectives: 49.5 us -> 38.8 us
  starting transfers between devices: 3.27 us -> 8.05 us
  waiting for transfers between devices: 0.82 us -> 3.89 us
  Pallas kernels: 13 us -> 13.9 us
    all_to_all x1, blocking collectives: 26.8 us -> 15.9 us  [on_device(): lax.all_to_all(folded, 'member', 0, 0, axis_index_groups=columns_of, tile...]
    ppermute x0 -> x3, starting transfers between devices: none -> 4.77 us  [on_device(): lax.ppermute(sent[d - 1], 'member', [(i, i // NEAR * NEAR + (i + d) % NEA...]
    ppermute x0 -> x3, waiting for transfers between devices: none -> 3.07 us  [on_device(): lax.ppermute(sent[d - 1], 'member', [(i, i // NEAR * NEAR + (i + d) % NEA...]
    pallas_call x1 -> x3, Pallas kernels: 6.2 us -> 7.11 us  [the longest x1 5.51 us: on_device(): pl.pallas_call(product_kernel, out_shape=(pltpu.VMEM((blocks, vectors, ti...]
  transfers between devices with their start and end apart: 2 -> 5, of which waited for: 1 -> 2; matrix products, arithmetic and copies ran while one was open for 0% -> 0% of each run, Pallas kernels for 6% -> 8%
where the time goes in v4:
time: 66.3 us; the launch traced here: 66 us
  blocking collectives  38.8 us (59%)
  Pallas kernels  13.9 us (21%)
  starting transfers between devices  8.05 us (12%)
  waiting for transfers between devices  3.89 us (6%)
  local copies, waits for them, and re-layouts  0.72 us (1%)
  between operations  0.7 us (1%)
    all_to_all x1, blocking collectives, on_device(): lax.all_to_all(sums.reshape(devices, 1, 128), ('member', 'slab'), 0, 0, t...  22.9 us
    all_to_all x1, blocking collectives, on_device(): lax.all_to_all(folded, 'member', 0, 0, axis_index_groups=columns_of, tile...  15.9 us
    pallas_call x1, Pallas kernels, on_device(): pl.pallas_call(product_kernel, out_shape=(pltpu.VMEM((blocks, vectors, ti...  5.51 us
    ppermute x3, starting transfers between devices, on_device(): lax.ppermute(sent[d - 1], 'member', [(i, i // NEAR * NEAR + (i + d) % NEA...  4.77 us
    pallas_call x1, Pallas kernels, on_device(): pl.pallas_call(functools.partial(stage_kernel, mem_dev=mem_dev), out_shap...  3.88 us
    ppermute x3, waiting for transfers between devices, on_device(): lax.ppermute(sent[d - 1], 'member', [(i, i // NEAR * NEAR + (i + d) % NEA...  3.07 us
    ppermute x1, starting transfers between devices, on_device(): lax.ppermute(high, 'slab', [(i, (i + 1) % slabs) for i in range(slabs)])  2.61 us
    pallas_call x1, Pallas kernels, on_device(): pl.pallas_call(edge_kernel, out_shape=(pltpu.VMEM(edge, BF16), pltpu.VMEM...  1.54 us
  transfers between devices with their start and end apart: 5, of which 2 were waited for; matrix products, arithmetic and copies ran while one was open for 0% of the time, Pallas kernels for 8%

profile of v4, /device:TPU:1, one launch (start us, length us, event | category | flops | bytes accessed | tf_op | source)
XLA Modules:
  0.0 66.0 jit_solution(7418524742810667599)
XLA Ops:
  0.6 1.5 %edge.1 = (bf16[16,8192]{1,0:T(8,128)(2,1)S(1)}, bf16[16,8192]{1,0:T(8,128)(2,1)S(1)}, bf16[2,32,8192]{2,1,0:T(8,128)(2,1)S(1)}) custom-call(bf16[2,32,8192]{2,1,0:T(8,128)(2,1)} %members_hbm.1, f32[32,8192]{1,0:T(8,128)} %direction_hbm.3), custom_call_target="tpu_custom_call" | custom-call | tf_op jit(solution)/shard_map/edge/pallas_call | solution.py:268
  2.2 2.6 %collective-permute-start = (bf16[16,8192]{1,0:T(8,128)(2,1)S(1)}, bf16[16,8192]{1,0:T(8,128)(2,1)S(1)}, u32[]{:S(2)}, u32[]{:S(2)}) collective-permute-start(bf16[16,8192]{1,0:T(8,128)(2,1)S(1)} %get-tuple-element.22), channel_id=1, source_target_pairs={{0,1},{1,2},{2,3},{3,4},{4,5},{5,6},{6,7},{7,0},{8,9},{9,10},{10,1... | collective-permute-start | bytes 786440 | tf_op jit(solution)/shard_map/ppermute | solution.py:277
  4.8 0.7 %collective-permute-start.1 = (bf16[16,8192]{1,0:T(8,128)(2,1)S(1)}, bf16[16,8192]{1,0:T(8,128)(2,1)S(1)}, u32[]{:S(2)}, u32[]{:S(2)}) collective-permute-start(bf16[16,8192]{1,0:T(8,128)(2,1)S(1)} %get-tuple-element.23), channel_id=1, source_target_pairs={{1,0},{2,1},{3,2},{4,3},{5,4},{6,5},{7,6},{0,7},{9,8},{10,9},{11,1... | collective-permute-start | bytes 786440 | tf_op jit(solution)/shard_map/ppermute | solution.py:278
  5.5 0.0 copy-start
  5.5 0.7 %copy-done = f32[256,9]{0,1:T(8,128)S(1)} copy-done((f32[256,9]{0,1:T(8,128)S(1)}, f32[256,9]{0,1:T(8,128)}, u32[]{:S(2)}) %copy-start) | copy-done | bytes 9240
  6.2 3.9 %stage.1 = (bf16[64,4,128,128]{3,2,1,0:T(8,128)(2,1)S(1)}, f32[32,8192]{1,0:T(8,128)S(1)}, f32[32,256]{1,0:T(8,128)S(1)}, f32[32,256]{1,0:T(8,128)S(1)}, f32[32,...) custom-call(f32[9,256]{1,0:T(8,128)S(1)} %bitcast.8, f32[32,8192]{1,0:T(8,128)} %direction_hbm.3, ...), custom_call_target="tpu_custom_call" | custom-call | bytes 16777216 | tf_op jit(solution)/shard_map/stage/pallas_call | solution.py:280
  10.1 0.0 collective-permute-done.below_ref
  10.1 0.8 %collective-permute-done.1.above_ref = bf16[16,8192]{1,0:T(8,128)(2,1)S(1)} collective-permute-done((bf16[16,8192]{1,0:T(8,128)(2,1)S(1)}, bf16[16,8192]{1,0:T(8,128)(2,1)S(1)}, u32[]{:S(2)}, u32[]{:S(2)}) %collective-permute-start.1) | collective-permute-done | bytes 262176 | tf_op jit(solution)/shard_map/ppermute | solution.py:278
  10.9 5.5 %product.1 = (bf16[64,64,128]{2,1,0:T(8,128)(2,1)S(1)}, bf16[8,32,256]{2,1,0:T(8,128)(2,1)S(1)}, bf16[8,32,256]{2,1,0:T(8,128)(2,1)S(1)}, bf16[8,32,256]{2,1,0:T(8,128)(2,1)S(1)}) custom-call(s32[4,64]{1,0:T(4,128)} %bitcast.9, bf16[192,96]{1,0:T(8,128)(2,1)S(1)} %get-tuple-element.20.band_ref, bf16[2,32,8192]{2,1,0:T(8,128)(2,1)S(1)} %get-tuple-element.18.members_ref, ...), custom_call_target="tpu_custom_call" | custom-call | tf_op jit(solution)/shard_map/product/pallas_call | solution.py:302
  16.4 1.1 %collective-permute-start.2 = (bf16[8,32,256]{2,1,0:T(8,128)(2,1)S(1)}, bf16[8,32,256]{2,1,0:T(8,128)(2,1)S(1)}, u32[]{:S(2)}, u32[]{:S(2)}) collective-permute-start(bf16[8,32,256]{2,1,0:T(8,128)(2,1)S(1)} %get-tuple-element.25), channel_id=1, source_target_pairs={{0,8},{8,16},{16,24},{24,0},{32,40},{40,48},{48,56},{56,32},{64,72... | collective-permute-start | bytes 393224 | tf_op jit(solution)/shard_map/ppermute | solution.py:316
  17.5 2.6 %collective-permute-start.3 = (bf16[8,32,256]{2,1,0:T(8,128)(2,1)S(1)}, bf16[8,32,256]{2,1,0:T(8,128)(2,1)S(1)}, u32[]{:S(2)}, u32[]{:S(2)}) collective-permute-start(bf16[8,32,256]{2,1,0:T(8,128)(2,1)S(1)} %get-tuple-element.26), channel_id=1, source_target_pairs={{0,16},{8,24},{16,0},{24,8},{32,48},{40,56},{48,32},{56,40},{64,80... | collective-permute-start | bytes 393224 | tf_op jit(solution)/shard_map/ppermute | solution.py:316
  20.1 1.1 %collective-permute-start.4 = (bf16[8,32,256]{2,1,0:T(8,128)(2,1)S(1)}, bf16[8,32,256]{2,1,0:T(8,128)(2,1)S(1)}, u32[]{:S(2)}, u32[]{:S(2)}) collective-permute-start(bf16[8,32,256]{2,1,0:T(8,128)(2,1)S(1)} %get-tuple-element.27), channel_id=1, source_target_pairs={{0,24},{8,0},{16,8},{24,16},{32,56},{40,32},{48,40},{56,48},{64,88... | collective-permute-start | bytes 393224 | tf_op jit(solution)/shard_map/ppermute | solution.py:316
  21.2 1.5 %own.1.own_ref = f32[8,32,256]{2,1,0:T(8,128)S(1)} custom-call(s32[4,64]{1,0:T(4,128)} %bitcast.10, bf16[2,32,8192]{2,1,0:T(8,128)(2,1)S(1)} %get-tuple-element.18.members_ref, bf16[64,4,128,128]{3,2,1,0:T(8,128)(2,1)S(1)} %get-tuple-element.19.tiles_ref, bf16[64,64,128]{2,1,0:T(8,128)(2,1)S(1)} %get-tuple-element.24.back_ref), custom_call_target="tpu_custom_call" | custom-call | flops 134217728 | bytes 2097152 | tf_op jit(solution)/shard_map/own/pallas_call | solution.py:321
  22.7 0.0 collective-permute-done.2.refs_0_
  22.7 3.1 %collective-permute-done.3.refs_1_ = bf16[8,32,256]{2,1,0:T(8,128)(2,1)S(1)} collective-permute-done((bf16[8,32,256]{2,1,0:T(8,128)(2,1)S(1)}, bf16[8,32,256]{2,1,0:T(8,128)(2,1)S(1)}, u32[]{:S(2)}, u32[]{:S(2)}) %collective-permute-start.3) | collective-permute-done | bytes 131104 | tf_op jit(solution)/shard_map/ppermute | solution.py:316
  25.8 0.0 collective-permute-done.4.refs_2_
  25.8 0.1 fold.1
  25.9 15.9 %all_to_all.10.parts_ref = bf16[8,32,256]{2,1,0:T(8,128)(2,1)S(1)} all-to-all(bf16[8,32,256]{2,1,0:T(8,128)(2,1)S(1)} %fold.1), channel_id=1, replica_groups={{0,32,64,96,128,160,192,224},{8,40,72,104,136,168,200,232},{16,48,80,11..., dimensions={0} | all-to-all | bytes 262144 | tf_op jit(solution)/shard_map/all_to_all | solution.py:340
  41.8 0.2 image.1
  42.0 22.9 %all_to_all.11 = f32[256,1,128]{2,1,0:T(1,128)S(1)} all-to-all(f32[256,1,128]{2,1,0:T(1,128)S(1)} %bitcast.7), channel_id=1, replica_groups=mesh['member'=32,'slab'=8] {'member','slab'}, dimensions={0} | all-to-all | bytes 262144 | tf_op jit(solution)/shard_map/all_to_all | solution.py:351
  64.9 1.2 %update.1 = (f32[32,256]{1,0:T(8,128)}, f32[32,256]{1,0:T(8,128)}, f32[32,256]{1,0:T(8,128)}) custom-call(f32[256,128]{1,0:T(8,128)S(1)} %bitcast.6, f32[32,256]{1,0:T(8,128)S(1)} %get-tuple-element.28.own_ref, f32[32,256]{1,0:T(8,128)S(1)} %get-tuple-element.29.residual_ref, f32[32,256]{1,0:T(8,128)S(1)} %get-tuple-element.31.iterate_ref, ...), custom_call_target="tpu_custom_call" | custom-call | tf_op jit(solution)/shard_map/update/pallas_call | solution.py:353
Async XLA Ops:
  2.2 7.9 %collective-permute-start = (bf16[16,8192]{1,0:T(8,128)(2,1)S(1)}, bf16[16,8192]{1,0:T(8,128)(2,1)S(1)}, u32[]{:S(2)}, u32[]{:S(2)}) collective-permute-start(bf16[16,8192]{1,0:T(8,128)(2,1)S(1)} %get-tuple-element.22), channel_id=1, source_target_pairs={{0,1},{1,2},{2,3},{3,4},{4,5},{5,6},{6,7},{7,0},{8,9},{9,10},{10,1... | collective-permute-start | bytes 786440 | tf_op jit(solution)/shard_map/ppermute | solution.py:277
  4.8 6.1 %collective-permute-start.1 = (bf16[16,8192]{1,0:T(8,128)(2,1)S(1)}, bf16[16,8192]{1,0:T(8,128)(2,1)S(1)}, u32[]{:S(2)}, u32[]{:S(2)}) collective-permute-start(bf16[16,8192]{1,0:T(8,128)(2,1)S(1)} %get-tuple-element.23), channel_id=1, source_target_pairs={{1,0},{2,1},{3,2},{4,3},{5,4},{6,5},{7,6},{0,7},{9,8},{10,9},{11,1... | collective-permute-start | bytes 786440 | tf_op jit(solution)/shard_map/ppermute | solution.py:278
  5.5 0.7 %copy-start = (f32[256,9]{0,1:T(8,128)S(1)}, f32[256,9]{0,1:T(8,128)}, u32[]{:S(2)}) copy-start(f32[256,9]{0,1:T(8,128)} %param.13) | copy-start | bytes 27652
  16.4 6.3 %collective-permute-start.2 = (bf16[8,32,256]{2,1,0:T(8,128)(2,1)S(1)}, bf16[8,32,256]{2,1,0:T(8,128)(2,1)S(1)}, u32[]{:S(2)}, u32[]{:S(2)}) collective-permute-start(bf16[8,32,256]{2,1,0:T(8,128)(2,1)S(1)} %get-tuple-element.25), channel_id=1, source_target_pairs={{0,8},{8,16},{16,24},{24,0},{32,40},{40,48},{48,56},{56,32},{64,72... | collective-permute-start | bytes 393224 | tf_op jit(solution)/shard_map/ppermute | solution.py:316
  17.5 8.3 %collective-permute-start.3 = (bf16[8,32,256]{2,1,0:T(8,128)(2,1)S(1)}, bf16[8,32,256]{2,1,0:T(8,128)(2,1)S(1)}, u32[]{:S(2)}, u32[]{:S(2)}) collective-permute-start(bf16[8,32,256]{2,1,0:T(8,128)(2,1)S(1)} %get-tuple-element.26), channel_id=1, source_target_pairs={{0,16},{8,24},{16,0},{24,8},{32,48},{40,56},{48,32},{56,40},{64,80... | collective-permute-start | bytes 393224 | tf_op jit(solution)/shard_map/ppermute | solution.py:316
  20.1 5.7 %collective-permute-start.4 = (bf16[8,32,256]{2,1,0:T(8,128)(2,1)S(1)}, bf16[8,32,256]{2,1,0:T(8,128)(2,1)S(1)}, u32[]{:S(2)}, u32[]{:S(2)}) collective-permute-start(bf16[8,32,256]{2,1,0:T(8,128)(2,1)S(1)} %get-tuple-element.27), channel_id=1, source_target_pairs={{0,24},{8,0},{16,8},{24,16},{32,56},{40,32},{48,40},{56,48},{64,88... | collective-permute-start | bytes 393224 | tf_op jit(solution)/shard_map/ppermute | solution.py:316

commit v5 on v3

v5 whole, which is shorter than its diff:
```python
import functools

import jax
import jax.numpy as jnp
from jax import lax
from jax.experimental import pallas as pl
from jax.experimental.pallas import tpu as pltpu
from jax.sharding import PartitionSpec as P

REACH = 4
HALO = 2 * REACH
EDGE_CHUNKS = 2
EARLY_SHARE = 2
LATE_CHUNKS = 6
LANES = 128
NEAR = 4
F32 = jnp.float32
BF16 = jnp.bfloat16
NT = (((1,), (1,)), ((), ()))
VMEM = pl.BlockSpec(memory_space=pltpu.VMEM)
HBM = pl.BlockSpec(memory_space=pltpu.HBM)


def link_kernel(members_hbm, direction_hbm, link_ref, part_ref, rim_ref, sems):
    mem_dev, near_rows, points = part_ref.shape
    lev_dev = direction_hbm.shape[0]
    step = points // EDGE_CHUNKS
    odd = lax.axis_index("slab") % 2
    first = pl.multiple_of(odd * (lev_dev - near_rows), near_rows)
    first_rim = pl.multiple_of(odd * (lev_dev - HALO), HALO)

    def copies(i):
        cols = pl.ds(i * step, step)
        return (
            pltpu.make_async_copy(direction_hbm.at[pl.ds(first_rim, HALO), cols], rim_ref.at[:, cols], sems.at[2 * i]),
            pltpu.make_async_copy(
                members_hbm.at[:, pl.ds(first, near_rows), cols], part_ref.at[:, :, cols], sems.at[2 * i + 1]
            ),
        )

    for i in range(EDGE_CHUNKS):
        for copy in copies(i):
            copy.start()
    for i in range(EDGE_CHUNKS):
        for copy in copies(i):
            copy.wait()
        cols = slice(i * step, (i + 1) * step)
        rows = []
        for m in range(mem_dev):
            near = part_ref[m, :, cols].astype(F32)
            rows.append(jnp.where(odd == 1, near[near_rows - HALO :], near[:HALO]) * rim_ref[:, cols])
        link_ref[:, cols] = jnp.concatenate(rows, axis=0).astype(BF16)


def split3(value):
    high = value.astype(BF16)
    rest = value - high.astype(F32)
    middle = rest.astype(BF16)
    low = (rest - middle.astype(F32)).astype(BF16)
    return jnp.concatenate([high, middle, low], axis=0)


def level_matrix(band, even, level_start, levels, lev_dev, mem_dev):
    span = band.shape[0]
    lanes = 128
    row = lax.broadcasted_iota(jnp.int32, (span, lanes), 0)
    col = lax.broadcasted_iota(jnp.int32, (span, lanes), 1)
    dense = jnp.zeros((span, lanes), F32)
    for offset in range(2 * REACH + 1):
        dense = jnp.where(col == row + offset, band[:, offset : offset + 1], dense)
    level = col + (level_start - HALO - REACH)
    dense = jnp.where((level >= 0) & (level < levels), dense, 0.0)
    own, low, high = dense[HALO : HALO + lev_dev], dense[:HALO], dense[HALO + lev_dev :]
    chip, link = jnp.where(even, high, low), jnp.where(even, low, high)
    rows = jnp.concatenate([own] * mem_dev, axis=0)
    cols = jnp.concatenate([own] * mem_dev + [chip] * mem_dev + [link] * mem_dev, axis=0)
    both = lax.dot_general(rows, cols, NT, precision=lax.Precision.HIGHEST, preferred_element_type=F32)
    i = lax.broadcasted_iota(jnp.int32, both.shape, 0)
    j = lax.broadcasted_iota(jnp.int32, both.shape, 1)
    keep = jnp.zeros(both.shape, jnp.bool_)
    vectors = mem_dev * lev_dev
    for m in range(mem_dev):
        mine = (i >= m * lev_dev) & (i < (m + 1) * lev_dev)
        theirs = (j >= m * lev_dev) & (j < (m + 1) * lev_dev)
        for first in (vectors + m * HALO, vectors + (mem_dev + m) * HALO):
            theirs = theirs | ((j >= first) & (j < first + HALO))
        keep = keep | (mine & theirs)
    both = jnp.where(keep, both, 0.0)
    inner, rim = [], []
    for m in range(mem_dev):
        first, last = m * lev_dev, (m + 1) * lev_dev
        inner.append(both[first + HALO : last - HALO])
        rim += [both[first : first + HALO], both[last - HALO : last]]
    return jnp.concatenate(inner, axis=0)[:, :vectors], jnp.concatenate(rim, axis=0)


def vertical_pass(band, fields, blocks, tile, smooth_ref, acc_ref=None):
    rows = band.shape[0] // 3

    def step(g, carry):
        cols = pl.ds(pl.multiple_of(g * 2 * tile, 2 * tile), 2 * tile)
        three = jnp.dot(band, fields(cols), preferred_element_type=F32)
        total = (three[2 * rows :] + three[rows : 2 * rows]) + three[:rows]
        total = total.astype(BF16)
        for k in range(2):
            smooth_ref[2 * g + k] = total[:, k * tile : (k + 1) * tile]
            if acc_ref is not None:
                acc_ref[2 * g + k] = jnp.zeros((rows, tile), F32)
        return carry

    lax.fori_loop(0, blocks // 2, step, 0, unroll=16)


def adjoint_pass(first, last, base, columns_ref, tiles_ref, smooth_ref, acc_ref, unroll):
    per_row, tile = tiles_ref.shape[1], tiles_ref.shape[3]

    def step(r, carry):
        where = [columns_ref[j, r] for j in range(per_row)]
        right = jnp.concatenate([tiles_ref[r - base, j] for j in range(per_row)], axis=1)
        spread = jnp.dot(smooth_ref[r], right, preferred_element_type=F32)
        new = [acc_ref[where[j]] + spread[:, j * tile : (j + 1) * tile] for j in range(per_row)]
        for j in range(per_row):
            acc_ref[where[j]] = new[j]
        return carry

    lax.fori_loop(first, last, step, 0, unroll=unroll)


def smooth_kernel(
    vertical_hbm, direction_hbm, members_hbm, residual_hbm, iterate_hbm, columns_hbm, tiles_hbm,
    members_ref, mixed_ref, residual_ref, iterate_ref, own_ref, band_ref, table_ref, smooth_ref, chip_ref, tiles_ref,
    vertical_ref, padded_ref, direction_ref, sems,
):
    mem_dev, lev_dev, points = members_ref.shape
    blocks, _, tile = smooth_ref.shape
    share = own_ref.shape[1]
    mine = pl.ds(pl.multiple_of(lax.axis_index("member") * share, share), share)
    pairs = [
        (vertical_hbm, vertical_ref),
        (direction_hbm, direction_ref),
        (members_hbm, members_ref),
        (columns_hbm, table_ref),
        (tiles_hbm.at[pl.ds(0, tiles_ref.shape[0])], tiles_ref),
        (direction_hbm.at[:, mine], own_ref),
        (residual_hbm, residual_ref),
        (iterate_hbm, iterate_ref),
    ]
    copies = [pltpu.make_async_copy(source, target, sems.at[i]) for i, (source, target) in enumerate(pairs)]
    for copy in copies:
        copy.start()
    width, levels = vertical_ref.shape
    slab = lax.axis_index("slab")
    level_start = slab * lev_dev
    even = slab % 2 == 0
    padded_ref[...] = jnp.zeros_like(padded_ref)
    copies[0].wait()
    for i in range(width):
        padded_ref[i : i + 1, LANES : LANES + levels] = vertical_ref[i : i + 1, :]
    total = padded_ref.shape[1]
    turned = pltpu.roll(padded_ref[...], total - (LANES - HALO + level_start), 1)[:, :LANES]
    band = jnp.concatenate([turned, jnp.zeros((LANES - turned.shape[0], LANES), F32)], axis=0).T
    inner, rim = level_matrix(band[: lev_dev + 2 * HALO], even, level_start, levels, lev_dev, mem_dev)
    band_ref[...] = split3(rim)
    copies[1].wait()
    copies[2].wait()

    def fields(cols):
        field = direction_ref[:, cols]
        wide = [members_ref[m, :, cols].astype(F32) * field for m in range(mem_dev)]
        low = jnp.concatenate([x[:HALO] for x in wide], axis=0)
        high = jnp.concatenate([x[lev_dev - HALO :] for x in wide], axis=0)
        chip_ref[:, cols] = jnp.where(even, high, low).astype(BF16)
        mixed = jnp.concatenate(wide, axis=0).astype(BF16)
        mixed_ref[:, cols] = mixed
        return mixed

    vertical_pass(split3(inner), fields, blocks, tile, smooth_ref)
    for copy in copies[3:]:
        copy.wait()


def interior_kernel(table_ref, smooth_ref, early_ref, tiles_hbm, late_ref, inner_ref, columns_ref, acc_ref, sems):
    early, late = early_ref.shape[0], late_ref.shape[0]
    part = late // LATE_CHUNKS
    copies = [
        pltpu.make_async_copy(
            tiles_hbm.at[pl.ds(early + i * part, part)], late_ref.at[pl.ds(i * part, part)], sems.at[i]
        )
        for i in range(LATE_CHUNKS)
    ]
    fetch = pltpu.make_async_copy(table_ref, columns_ref, sems.at[LATE_CHUNKS])
    fetch.start()
    for copy in copies:
        copy.start()
    acc_ref[...] = jnp.zeros_like(acc_ref)
    fetch.wait()
    adjoint_pass(0, early, 0, columns_ref, early_ref, smooth_ref, acc_ref, 8)
    for i, copy in enumerate(copies):
        copy.wait()
        adjoint_pass(early + i * part, early + (i + 1) * part, early, columns_ref, late_ref, smooth_ref, acc_ref, 8)
    inner_ref[...] = acc_ref[...].astype(BF16)


def forward_share(g, wide, base, columns_ref, tiles_ref, inner_ref, rim_ref, members_ref):
    mem_dev, lev_dev, points = members_ref.shape
    blocks, per_row, tile, _ = tiles_ref.shape
    middle = lev_dev - 2 * HALO
    pieces = []
    for k in range(wide):
        r = g * wide + k
        left = []
        for j in range(per_row):
            c = columns_ref[j, r]
            left.append(jnp.concatenate([inner_ref[c], rim_ref[c]], axis=0))
        right = jnp.concatenate([tiles_ref[r - base, j] for j in range(per_row)], axis=1)
        field = lax.dot_general(jnp.concatenate(left, axis=1), right, NT, preferred_element_type=F32)
        cols = pl.ds(pl.multiple_of(r * tile, tile), tile)
        total = jnp.zeros((lev_dev, tile), F32)
        for m in range(mem_dev):
            inside = field[m * middle : (m + 1) * middle]
            low = mem_dev * middle + 2 * m * HALO
            levels = jnp.concatenate([field[low : low + HALO], inside, field[low + HALO : low + 2 * HALO]], axis=0)
            total = total + members_ref[m, :, cols].astype(F32) * levels
        pieces.append(total)
    return jnp.concatenate(pieces, axis=1)


def forward_shares(shifts, columns_ref, early_ref, late_ref, inner_ref, rim_ref, members_ref, out_refs):
    far_count, _, share = out_refs[0].shape
    early = early_ref.shape[0]
    wide = share // early_ref.shape[3]
    here = lax.axis_index("member") % NEAR
    for shift, out_ref in zip(shifts, out_refs):
        target = (here + shift) % NEAR
        for z in range(far_count):
            in_early = (z + 1) * NEAR * wide <= early
            base, tiles_ref = (0, early_ref) if in_early else (early, late_ref)
            value = forward_share(z * NEAR + target, wide, base, columns_ref, tiles_ref, inner_ref, rim_ref, members_ref)
            out_ref[z] = value.astype(out_ref.dtype)


def product_kernel(
    table_ref, band_ref, members_ref, mixed_ref, inner_ref, chip_ref, link_ref, early_ref, late_ref,
    rim_ref, *rest, shifts,
):
    *out_refs, columns_ref, smooth_ref, acc_ref, sem = rest
    early, _, tile, _ = early_ref.shape
    blocks = early + late_ref.shape[0]
    fetch = pltpu.make_async_copy(table_ref, columns_ref, sem)
    fetch.start()

    def fields(cols):
        return jnp.concatenate([mixed_ref[:, cols], chip_ref[:, cols], link_ref[:, cols]], axis=0)

    vertical_pass(band_ref[...], fields, blocks, tile, smooth_ref, acc_ref)
    fetch.wait()
    adjoint_pass(0, early, 0, columns_ref, early_ref, smooth_ref, acc_ref, 16)
    adjoint_pass(early, blocks, early, columns_ref, late_ref, smooth_ref, acc_ref, 16)
    rim_ref[...] = acc_ref[...].astype(BF16)
    forward_shares(shifts, columns_ref, early_ref, late_ref, inner_ref, rim_ref, members_ref, out_refs)


def share_kernel(table_ref, members_ref, early_ref, late_ref, inner_ref, rim_ref, *rest, shifts):
    *out_refs, columns_ref, sem = rest
    fetch = pltpu.make_async_copy(table_ref, columns_ref, sem)
    fetch.start()
    fetch.wait()
    forward_shares(shifts, columns_ref, early_ref, late_ref, inner_ref, rim_ref, members_ref, out_refs)


def fold_kernel(own_ref, *refs):
    *arrived, out_ref = refs
    total = own_ref[...]
    for ref in arrived:
        total = total + ref[...].astype(F32)
    out_ref[...] = total.astype(out_ref.dtype)


def full_sum(value):
    return jnp.sum(jnp.sum(value, axis=0, keepdims=True), axis=1, keepdims=True)


def image_kernel(parts_ref, own_ref, residual_ref, image_ref, sums_ref, *, scale):
    total = parts_ref[0].astype(F32)
    for i in range(1, parts_ref.shape[0]):
        total = total + parts_ref[i].astype(F32)
    own = own_ref[...]
    residual = residual_ref[...]
    image = own + total / scale
    image_ref[...] = image
    rr = full_sum(residual * residual)
    di = full_sum(own * image)
    ii = full_sum(image * image)
    ri = full_sum(residual * image)
    guess = jnp.where(ii > 0.0, ri / jnp.where(ii > 0.0, ii, 1.0), 0.0)
    left = residual - guess * image
    ll = full_sum(left * left)
    li = full_sum(left * image)
    lane = lax.broadcasted_iota(jnp.int32, (1, sums_ref.shape[1]), 1)
    row = jnp.zeros(lane.shape, F32)
    for k, value in enumerate((rr, di, ll, li, ii, guess)):
        row = jnp.where(lane == k, value, row)
    sums_ref[...] = jnp.broadcast_to(row, sums_ref.shape)


def update_kernel(parts_ref, own_ref, residual_ref, iterate_ref, image_ref, x_ref, r_ref, d_ref):
    parts = parts_ref[...]
    sums = jnp.sum(parts, axis=0, keepdims=True)
    norm_old = sums[:, 0:1]
    alpha = norm_old / sums[:, 1:2]
    ll, li, ii, guess = (parts[:, k : k + 1] for k in range(2, 6))
    shift = guess - alpha
    norm_new = jnp.sum(ll + shift * (2.0 * li + shift * ii), axis=0, keepdims=True)
    own = own_ref[...]
    residual_new = residual_ref[...] - alpha * image_ref[...]
    x_ref[...] = iterate_ref[...] + alpha * own
    r_ref[...] = residual_new
    d_ref[...] = residual_new + (norm_new / norm_old) * own


def on_device(members, direction, residual, iterate, tiles, columns, vertical):
    mem_dev, lev_dev, points = members.shape
    blocks, per_row, tile = tiles.shape[:3]
    vectors = mem_dev * lev_dev
    groups, slabs = lax.axis_size("member"), lax.axis_size("slab")
    share = points // groups
    member_count = mem_dev * groups
    levels, width = vertical.shape
    square = (lev_dev, share)
    edge = (mem_dev * HALO, points)

    far = functools.partial(pltpu.with_memory_space_constraint, memory_space=pltpu.HBM)
    near = functools.partial(pltpu.with_memory_space_constraint, memory_space=pltpu.VMEM)
    limit = pltpu.CompilerParams(vmem_limit_bytes=32 * 2**20)
    to_link, = pl.pallas_call(
        link_kernel,
        out_shape=(pltpu.VMEM(edge, BF16),),
        in_specs=[HBM, HBM],
        out_specs=(VMEM,),
        scratch_shapes=[
            pltpu.VMEM((mem_dev, 2 * HALO, points), BF16),
            pltpu.VMEM((HALO, points), F32),
            pltpu.SemaphoreType.DMA((2 * EDGE_CHUNKS,)),
        ],
        compiler_params=limit,
        name="link_edge",
    )(far(members), far(direction))
    pairs = [(i, (i + 1) % slabs) for i in range(1, slabs, 2)]
    link = lax.ppermute(to_link, "slab", pairs + [(target, source) for source, target in pairs])

    rim_rows = 2 * mem_dev * HALO
    inner_rows = vectors - rim_rows
    columns_scratch = pltpu.SMEM((per_row, blocks), jnp.int32)
    early = EARLY_SHARE * blocks // 8
    late = blocks - early
    (
        members_near, mixed, residual_near, iterate_near, own, band, columns_near, smooth, to_chip, tiles_early,
    ) = pl.pallas_call(
        smooth_kernel,
        out_shape=(
            pltpu.VMEM(members.shape, BF16), pltpu.VMEM((vectors, points), BF16),
            pltpu.VMEM(square, F32), pltpu.VMEM(square, F32), pltpu.VMEM(square, F32),
            pltpu.VMEM((3 * rim_rows, vectors + rim_rows), BF16),
            pltpu.VMEM((per_row, blocks), jnp.int32),
            pltpu.VMEM((blocks, inner_rows, tile), BF16),
            pltpu.VMEM(edge, BF16),
            pltpu.VMEM((early,) + tiles.shape[1:], BF16),
        ),
        in_specs=[HBM] * 7,
        out_specs=(VMEM,) * 10,
        scratch_shapes=[
            pltpu.VMEM((width, levels), F32),
            pltpu.VMEM((-(-width // 8) * 8, levels + 2 * LANES), F32),
            pltpu.VMEM(direction.shape, F32),
            pltpu.SemaphoreType.DMA((8,)),
        ],
        compiler_params=limit,
        cost_estimate=pl.CostEstimate(flops=0, bytes_accessed=tiles.size // 2, transcendentals=0),
        name="smooth",
    )(far(vertical.T), far(direction), far(members), far(residual), far(iterate), far(columns.T), far(tiles))
    chip = lax.ppermute(to_chip, "slab", [(i, i ^ 1) for i in range(slabs)])
    tiles_late, inner = pl.pallas_call(
        interior_kernel,
        out_shape=(pltpu.VMEM((late,) + tiles.shape[1:], BF16), pltpu.VMEM((blocks, inner_rows, tile), BF16)),
        in_specs=[VMEM] * 3 + [HBM],
        out_specs=(VMEM,) * 2,
        scratch_shapes=[
            columns_scratch,
            pltpu.VMEM((blocks, inner_rows, tile), F32),
            pltpu.SemaphoreType.DMA((LATE_CHUNKS + 1,)),
        ],
        compiler_params=limit,
        cost_estimate=pl.CostEstimate(
            flops=2 * inner_rows * points * per_row * tile, bytes_accessed=2 * tiles.size * 2, transcendentals=0
        ),
        name="interior",
    )(columns_near, smooth, tiles_early, far(tiles))

    far_count = groups // NEAR
    piece = (far_count, lev_dev, share)
    flops = 2 * vectors * points * per_row * tile

    def shares(shifts, dtype, name):
        return pl.pallas_call(
            functools.partial(share_kernel, shifts=shifts),
            out_shape=(pltpu.VMEM(piece, dtype),) * len(shifts),
            in_specs=[VMEM] * 6,
            out_specs=(VMEM,) * len(shifts),
            scratch_shapes=[columns_scratch, pltpu.SemaphoreType.DMA],
            compiler_params=limit,
            cost_estimate=pl.CostEstimate(
                flops=flops * len(shifts) // NEAR, bytes_accessed=tiles.size * 2 * len(shifts) // NEAR, transcendentals=0
            ),
            name=name,
        )(columns_near, members_near, tiles_early, tiles_late, inner, rim)

    def send(value, shift):
        return lax.ppermute(value, "member", [(i, i // NEAR * NEAR + (i + shift) % NEAR) for i in range(groups)])

    early, late = (1, 3, 2), ()
    rim, *sent = pl.pallas_call(
        functools.partial(product_kernel, shifts=early),
        out_shape=(pltpu.VMEM((blocks, rim_rows, tile), BF16),) + (pltpu.VMEM(piece, BF16),) * len(early),
        in_specs=[VMEM] * 9,
        out_specs=(VMEM,) * (1 + len(early)),
        scratch_shapes=[
            columns_scratch,
            pltpu.VMEM((blocks, rim_rows, tile), BF16),
            pltpu.VMEM((blocks, rim_rows, tile), F32),
            pltpu.SemaphoreType.DMA,
        ],
        compiler_params=limit,
        name="product",
    )(columns_near, band, members_near, mixed, inner, chip, link, tiles_early, tiles_late)
    arrived = [send(value, shift) for value, shift in zip(sent, early)]
    own_part, = shares((0,), F32, "own")
    folded = pl.pallas_call(
        fold_kernel,
        out_shape=pltpu.VMEM(piece, BF16),
        in_specs=[VMEM] * NEAR,
        out_specs=VMEM,
        compiler_params=limit,
        name="fold",
    )(near(own_part), *(near(x) for x in arrived))
    columns_of = [[y + NEAR * z for z in range(far_count)] for y in range(NEAR)]
    parts = lax.all_to_all(folded, "member", 0, 0, axis_index_groups=columns_of, tiled=True)
    devices = groups * slabs
    image, sums = pl.pallas_call(
        functools.partial(image_kernel, scale=float(member_count - 1)),
        out_shape=(pltpu.VMEM(square, F32), pltpu.VMEM((devices, 128), F32)),
        in_specs=[VMEM] * 3,
        out_specs=(VMEM,) * 2,
        compiler_params=limit,
        name="image",
    )(near(parts), own, residual_near)

    spread = lax.all_to_all(sums.reshape(devices, 1, 128), ("member", "slab"), 0, 0, tiled=True)
    field = jax.ShapeDtypeStruct(square, F32)
    return pl.pallas_call(
        update_kernel,
        out_shape=(field, field, field),
        in_specs=[VMEM] * 5,
        out_specs=(VMEM,) * 3,
        compiler_params=limit,
        name="update",
    )(near(spread.reshape(devices, 128)), own, residual_near, iterate_near, image)


def solution(mesh):
    placed = (
        P("member", "slab", None),
        P("slab", None),
        P("slab", "member"),
        P("slab", "member"),
        P(),
        P(),
        P(),
    )
    return jax.shard_map(
        on_device,
        mesh=mesh,
        in_specs=placed,
        out_specs=(P("slab", "member"), P("slab", "member"), P("slab", "member")),
        check_vma=False,
    )
```

time: 68.2 us -> 64.4 us (0.944)
  blocking collectives: 49.5 us -> 36.4 us
  starting transfers between devices: 3.27 us -> 8.34 us
  waiting for transfers between devices: 0.82 us -> 4.12 us
  Pallas kernels: 13 us -> 14.6 us
  local copies, waits for them, and re-layouts: 0.72 us -> 0 us
    all_to_all x1, blocking collectives: 26.8 us -> 16.2 us  [on_device(): lax.all_to_all(folded, 'member', 0, 0, axis_index_groups=columns_of, tile...]
    ppermute x2 -> x5, starting transfers between devices: 3.27 us -> 8.34 us  [the longest x3 4.46 us: send(): lax.ppermute(value, 'member', [(i, i // NEAR * NEAR + (i + shift) % NEAR)...]
    ppermute x2 -> x5, waiting for transfers between devices: 0.82 us -> 4.12 us  [the longest x3 4.11 us: send(): lax.ppermute(value, 'member', [(i, i // NEAR * NEAR + (i + shift) % NEAR)...]
    all_to_all x1, blocking collectives: 22.6 us -> 20.2 us  [on_device(): lax.all_to_all(sums.reshape(devices, 1, 128), ('member', 'slab'), 0, 0, t...]
    pallas_call x3 -> x6, Pallas kernels: 11.6 us -> 13.2 us  [the longest x1 4.87 us: on_device(): pl.pallas_call(functools.partial(product_kernel, shifts=early), out_shape...]
    unnamed x2 -> x0, local copies, waits for them, and re-layouts: 0.72 us -> none
  transfers between devices with their start and end apart: 2 -> 5, of which waited for: 1 -> 2; matrix products, arithmetic and copies ran while one was open for 0% -> 0% of each run, Pallas kernels for 6% -> 11%
where the time goes in v5:
time: 64.4 us; the launch traced here: 64.2 us
  blocking collectives  36.4 us (57%)
  Pallas kernels  14.6 us (23%)
  starting transfers between devices  8.34 us (13%)
  waiting for transfers between devices  4.12 us (6%)
  between operations  0.71 us (1%)
    all_to_all x1, blocking collectives, on_device(): lax.all_to_all(sums.reshape(devices, 1, 128), ('member', 'slab'), 0, 0, t...  20.2 us
    all_to_all x1, blocking collectives, on_device(): lax.all_to_all(folded, 'member', 0, 0, axis_index_groups=columns_of, tile...  16.2 us
    pallas_call x1, Pallas kernels, on_device(): pl.pallas_call(functools.partial(product_kernel, shifts=early), out_shape...  4.87 us
    ppermute x3, starting transfers between devices, send(): lax.ppermute(value, 'member', [(i, i // NEAR * NEAR + (i + shift) % NEAR)...  4.46 us
    ppermute x3, waiting for transfers between devices, send(): lax.ppermute(value, 'member', [(i, i // NEAR * NEAR + (i + shift) % NEAR)...  4.11 us
    pallas_call x1, Pallas kernels, on_device(): pl.pallas_call(interior_kernel, out_shape=(pltpu.VMEM((late,) + tiles.sha...  3.2 us
    ppermute x1, starting transfers between devices, on_device(): lax.ppermute(to_link, 'slab', pairs + [(target, source) for source, targe...  2.69 us
    pallas_call x1, Pallas kernels, on_device(): pl.pallas_call(smooth_kernel, out_shape=(pltpu.VMEM(members.shape, BF16),...  2.39 us
  transfers between devices with their start and end apart: 5, of which 2 were waited for; matrix products, arithmetic and copies ran while one was open for 0% of the time, Pallas kernels for 11%

profile of v5, /device:TPU:1, one launch (start us, length us, event | category | flops | bytes accessed | tf_op | source)
XLA Modules:
  0.0 64.2 jit_solution(12958573054901783680)
XLA Ops:
  0.6 1.3 %link_edge.1 = bf16[16,8192]{1,0:T(8,128)(2,1)S(1)} custom-call(bf16[2,32,8192]{2,1,0:T(8,128)(2,1)} %members_hbm.3, f32[32,8192]{1,0:T(8,128)} %direction_hbm.3), custom_call_target="tpu_custom_call" | custom-call | tf_op jit(solution)/shard_map/link_edge/pallas_call | solution.py:335
  1.9 2.7 %collective-permute-start.1 = (bf16[16,8192]{1,0:T(8,128)(2,1)S(1)}, bf16[16,8192]{1,0:T(8,128)(2,1)S(1)}, u32[]{:S(2)}, u32[]{:S(2)}) collective-permute-start(bf16[16,8192]{1,0:T(8,128)(2,1)S(1)} %link_edge.1), channel_id=1, source_target_pairs={{1,2},{3,4},{5,6},{7,0},{2,1},{4,3},{6,5},{0,7},{9,10},{11,12},{13... | collective-permute-start | bytes 786440 | tf_op jit(solution)/shard_map/ppermute | solution.py:349
  4.6 2.4 %smooth.1 = (bf16[2,32,8192]{2,1,0:T(8,128)(2,1)S(1)}, bf16[64,8192]{1,0:T(8,128)(2,1)S(1)}, f32[32,256]{1,0:T(8,128)S(1)}, f32[32,256]{1,0:T(8,128)S(1)}, f32[3...) custom-call(f32[9,256]{1,0:T(8,128)} %bitcast.8, ...), custom_call_target="tpu_custom_call" | custom-call | bytes 2097152 | tf_op jit(solution)/shard_map/smooth/pallas_call | solution.py:358
  7.0 1.2 %collective-permute-start = (bf16[16,8192]{1,0:T(8,128)(2,1)S(1)}, bf16[16,8192]{1,0:T(8,128)(2,1)S(1)}, u32[]{:S(2)}, u32[]{:S(2)}) collective-permute-start(bf16[16,8192]{1,0:T(8,128)(2,1)S(1)} %get-tuple-element.29), channel_id=1, source_target_pairs={{0,1},{1,0},{2,3},{3,2},{4,5},{5,4},{6,7},{7,6},{8,9},{9,8},{10,11... | collective-permute-start | bytes 786440 | tf_op jit(solution)/shard_map/ppermute | solution.py:381
  8.2 3.2 %interior.1 = (bf16[48,4,128,128]{3,2,1,0:T(8,128)(2,1)S(1)}, bf16[64,32,128]{2,1,0:T(8,128)(2,1)S(1)}) custom-call(s32[4,64]{1,0:T(4,128)S(1)} %get-tuple-element.21.table_ref, bf16[64,32,128]{2,1,0:T(8,128)(2,1)S(1)} %get-tuple-element.24.smooth_ref, bf16[16,4,128,128]{3,2,1,0:T(8,128)(2,1)S(1)} %get-tuple-element.23.early_ref, ...), custom_call_target="tpu_custom_call" | custom-call | flops 268435456 | bytes 16777216 | tf_op jit(solution)/shard_map/interior/pallas_call | solution.py:382
  11.4 0.0 collective-permute-done.1.link_ref
  11.4 0.0 collective-permute-done.chip_ref
  11.4 4.9 %product.1 = (bf16[64,32,128]{2,1,0:T(8,128)(2,1)S(1)}, bf16[8,32,256]{2,1,0:T(8,128)(2,1)S(1)}, bf16[8,32,256]{2,1,0:T(8,128)(2,1)S(1)}, bf16[8,32,256]{2,1,0:T(8,128)(2,1)S(1)}) custom-call(s32[4,64]{1,0:T(4,128)S(1)} %get-tuple-element.21.table_ref, bf16[96,96]{1,0:T(8,128)(2,1)S(1)} %get-tuple-element.27.band_ref, ...), custom_call_target="tpu_custom_call" | custom-call | tf_op jit(solution)/shard_map/product/pallas_call | solution.py:421
  16.3 1.4 %collective-permute-start.2 = (bf16[8,32,256]{2,1,0:T(8,128)(2,1)S(1)}, bf16[8,32,256]{2,1,0:T(8,128)(2,1)S(1)}, u32[]{:S(2)}, u32[]{:S(2)}) collective-permute-start(bf16[8,32,256]{2,1,0:T(8,128)(2,1)S(1)} %get-tuple-element.31), channel_id=1, source_target_pairs={{0,8},{8,16},{16,24},{24,0},{32,40},{40,48},{48,56},{56,32},{64,72... | collective-permute-start | bytes 393224 | tf_op jit(solution)/shard_map/ppermute | solution.py:418
  17.7 1.5 %collective-permute-start.3 = (bf16[8,32,256]{2,1,0:T(8,128)(2,1)S(1)}, bf16[8,32,256]{2,1,0:T(8,128)(2,1)S(1)}, u32[]{:S(2)}, u32[]{:S(2)}) collective-permute-start(bf16[8,32,256]{2,1,0:T(8,128)(2,1)S(1)} %get-tuple-element.32), channel_id=1, source_target_pairs={{0,24},{8,0},{16,8},{24,16},{32,56},{40,32},{48,40},{56,48},{64,88... | collective-permute-start | bytes 393224 | tf_op jit(solution)/shard_map/ppermute | solution.py:418
  19.2 1.6 %collective-permute-start.4 = (bf16[8,32,256]{2,1,0:T(8,128)(2,1)S(1)}, bf16[8,32,256]{2,1,0:T(8,128)(2,1)S(1)}, u32[]{:S(2)}, u32[]{:S(2)}) collective-permute-start(bf16[8,32,256]{2,1,0:T(8,128)(2,1)S(1)} %get-tuple-element.33), channel_id=1, source_target_pairs={{0,16},{8,24},{16,0},{24,8},{32,48},{40,56},{48,32},{56,40},{64,80... | collective-permute-start | bytes 393224 | tf_op jit(solution)/shard_map/ppermute | solution.py:418
  20.7 1.4 %own.1.own_ref = f32[8,32,256]{2,1,0:T(8,128)S(1)} custom-call(s32[4,64]{1,0:T(4,128)S(1)} %get-tuple-element.21.table_ref, bf16[2,32,8192]{2,1,0:T(8,128)(2,1)S(1)} %get-tuple-element.22.members_ref, bf16[16,4,128,128]{3,2,1,0:T(8,128)(2,1)S(1)} %get-tuple-element.23.early_ref, bf16[48,4,128,128]{3,2,1,0:T(8,128)(2,1)S(1)} %get-tuple-element.25.late_ref, ...), custom_call_target="tpu_custom_call" | custom-call | flops 134217728 | bytes 2097152 | tf_op jit(solution)/shard_map/own/pallas_call | solution.py:404
  22.2 0.0 collective-permute-done.2.refs_0_
  22.2 0.3 collective-permute-done.3.refs_1_
  22.5 3.8 %collective-permute-done.4.refs_2_ = bf16[8,32,256]{2,1,0:T(8,128)(2,1)S(1)} collective-permute-done((bf16[8,32,256]{2,1,0:T(8,128)(2,1)S(1)}, bf16[8,32,256]{2,1,0:T(8,128)(2,1)S(1)}, u32[]{:S(2)}, u32[]{:S(2)}) %collective-permute-start.4) | collective-permute-done | bytes 131104 | tf_op jit(solution)/shard_map/ppermute | solution.py:418
  26.3 0.1 fold.1
  26.4 16.2 %all_to_all.10.parts_ref = bf16[8,32,256]{2,1,0:T(8,128)(2,1)S(1)} all-to-all(bf16[8,32,256]{2,1,0:T(8,128)(2,1)S(1)} %fold.1), channel_id=1, replica_groups={{0,32,64,96,128,160,192,224},{8,40,72,104,136,168,200,232},{16,48,80,11..., dimensions={0} | all-to-all | bytes 262144 | tf_op jit(solution)/shard_map/all_to_all | solution.py:446
  42.5 0.2 image.1
  42.8 20.2 %all_to_all.11 = f32[256,1,128]{2,1,0:T(1,128)S(1)} all-to-all(f32[256,1,128]{2,1,0:T(1,128)S(1)} %bitcast.7), channel_id=1, replica_groups=mesh['member'=32,'slab'=8] {'member','slab'}, dimensions={0} | all-to-all | bytes 262144 | tf_op jit(solution)/shard_map/all_to_all | solution.py:457
  63.0 1.2 %update.1 = (f32[32,256]{1,0:T(8,128)}, f32[32,256]{1,0:T(8,128)}, f32[32,256]{1,0:T(8,128)}) custom-call(f32[256,128]{1,0:T(8,128)S(1)} %bitcast.6, f32[32,256]{1,0:T(8,128)S(1)} %get-tuple-element.34.own_ref, f32[32,256]{1,0:T(8,128)S(1)} %get-tuple-element.35.residual_ref, f32[32,256]{1,0:T(8,128)S(1)} %get-tuple-element.37.iterate_ref, ...), custom_call_target="tpu_custom_call" | custom-call | tf_op jit(solution)/shard_map/update/pallas_call | solution.py:459
Async XLA Ops:
  1.9 9.5 %collective-permute-start.1 = (bf16[16,8192]{1,0:T(8,128)(2,1)S(1)}, bf16[16,8192]{1,0:T(8,128)(2,1)S(1)}, u32[]{:S(2)}, u32[]{:S(2)}) collective-permute-start(bf16[16,8192]{1,0:T(8,128)(2,1)S(1)} %link_edge.1), channel_id=1, source_target_pairs={{1,2},{3,4},{5,6},{7,0},{2,1},{4,3},{6,5},{0,7},{9,10},{11,12},{13... | collective-permute-start | bytes 786440 | tf_op jit(solution)/shard_map/ppermute | solution.py:349
  7.0 4.4 %collective-permute-start = (bf16[16,8192]{1,0:T(8,128)(2,1)S(1)}, bf16[16,8192]{1,0:T(8,128)(2,1)S(1)}, u32[]{:S(2)}, u32[]{:S(2)}) collective-permute-start(bf16[16,8192]{1,0:T(8,128)(2,1)S(1)} %get-tuple-element.29), channel_id=1, source_target_pairs={{0,1},{1,0},{2,3},{3,2},{4,5},{5,4},{6,7},{7,6},{8,9},{9,8},{10,11... | collective-permute-start | bytes 786440 | tf_op jit(solution)/shard_map/ppermute | solution.py:381
  16.3 5.9 %collective-permute-start.2 = (bf16[8,32,256]{2,1,0:T(8,128)(2,1)S(1)}, bf16[8,32,256]{2,1,0:T(8,128)(2,1)S(1)}, u32[]{:S(2)}, u32[]{:S(2)}) collective-permute-start(bf16[8,32,256]{2,1,0:T(8,128)(2,1)S(1)} %get-tuple-element.31), channel_id=1, source_target_pairs={{0,8},{8,16},{16,24},{24,0},{32,40},{40,48},{48,56},{56,32},{64,72... | collective-permute-start | bytes 393224 | tf_op jit(solution)/shard_map/ppermute | solution.py:418
  17.7 4.8 %collective-permute-start.3 = (bf16[8,32,256]{2,1,0:T(8,128)(2,1)S(1)}, bf16[8,32,256]{2,1,0:T(8,128)(2,1)S(1)}, u32[]{:S(2)}, u32[]{:S(2)}) collective-permute-start(bf16[8,32,256]{2,1,0:T(8,128)(2,1)S(1)} %get-tuple-element.32), channel_id=1, source_target_pairs={{0,24},{8,0},{16,8},{24,16},{32,56},{40,32},{48,40},{56,48},{64,88... | collective-permute-start | bytes 393224 | tf_op jit(solution)/shard_map/ppermute | solution.py:418
  19.2 7.1 %collective-permute-start.4 = (bf16[8,32,256]{2,1,0:T(8,128)(2,1)S(1)}, bf16[8,32,256]{2,1,0:T(8,128)(2,1)S(1)}, u32[]{:S(2)}, u32[]{:S(2)}) collective-permute-start(bf16[8,32,256]{2,1,0:T(8,128)(2,1)S(1)} %get-tuple-element.33), channel_id=1, source_target_pairs={{0,16},{8,24},{16,0},{24,8},{32,48},{40,56},{48,32},{56,40},{64,80... | collective-permute-start | bytes 393224 | tf_op jit(solution)/shard_map/ppermute | solution.py:418

commit v6 on v5

--- a/solution.py
+++ b/solution.py
@@ -454,7 +454,9 @@
         name="image",
     )(near(parts), own, residual_near)
 
-    spread = lax.all_to_all(sums.reshape(devices, 1, 128), ("member", "slab"), 0, 0, tiled=True)
+    spread = lax.all_to_all(
+        sums.reshape(devices, 1, 128), ("member", "slab"), 0, 0, axis_index_groups=[list(range(devices))[::-1]], tiled=True
+    )
     field = jax.ShapeDtypeStruct(square, F32)
     return pl.pallas_call(
         update_kernel,

time: 64.4 us -> 64.2 us (level)
  no operation moved by 1% of the time
where the time goes in v6:
time: 64.2 us; the launch traced here: 63.9 us
  blocking collectives  36.2 us (56%)
  Pallas kernels  14.6 us (23%)
  starting transfers between devices  8.29 us (13%)
  waiting for transfers between devices  4.06 us (6%)
  between operations  0.71 us (1%)
    all_to_all x1, blocking collectives, on_device(): lax.all_to_all(sums.reshape(devices, 1, 128), ('member', 'slab'), 0, 0, a...  20 us
    all_to_all x1, blocking collectives, on_device(): lax.all_to_all(folded, 'member', 0, 0, axis_index_groups=columns_of, tile...  16.2 us
    pallas_call x1, Pallas kernels, on_device(): pl.pallas_call(functools.partial(product_kernel, shifts=early), out_shape...  4.92 us
    ppermute x3, starting transfers between devices, send(): lax.ppermute(value, 'member', [(i, i // NEAR * NEAR + (i + shift) % NEAR)...  4.42 us
    ppermute x3, waiting for transfers between devices, send(): lax.ppermute(value, 'member', [(i, i // NEAR * NEAR + (i + shift) % NEAR)...  4.06 us
    pallas_call x1, Pallas kernels, on_device(): pl.pallas_call(interior_kernel, out_shape=(pltpu.VMEM((late,) + tiles.sha...  3.2 us
    ppermute x1, starting transfers between devices, on_device(): lax.ppermute(to_link, 'slab', pairs + [(target, source) for source, targe...  2.69 us
    pallas_call x1, Pallas kernels, on_device(): pl.pallas_call(smooth_kernel, out_shape=(pltpu.VMEM(members.shape, BF16),...  2.39 us
  transfers between devices with their start and end apart: 5, of which 2 were waited for; matrix products, arithmetic and copies ran while one was open for 0% of the time, Pallas kernels for 11%

profile of v6, /device:TPU:1, one launch (start us, length us, event | category | flops | bytes accessed | tf_op | source)
XLA Modules:
  0.0 63.9 jit_solution(11533444986682096777)
XLA Ops:
  0.6 1.3 %link_edge.1 = bf16[16,8192]{1,0:T(8,128)(2,1)S(1)} custom-call(bf16[2,32,8192]{2,1,0:T(8,128)(2,1)} %members_hbm.3, f32[32,8192]{1,0:T(8,128)} %direction_hbm.3), custom_call_target="tpu_custom_call" | custom-call | tf_op jit(solution)/shard_map/link_edge/pallas_call | solution.py:335
  1.9 2.7 %collective-permute-start.1 = (bf16[16,8192]{1,0:T(8,128)(2,1)S(1)}, bf16[16,8192]{1,0:T(8,128)(2,1)S(1)}, u32[]{:S(2)}, u32[]{:S(2)}) collective-permute-start(bf16[16,8192]{1,0:T(8,128)(2,1)S(1)} %link_edge.1), channel_id=1, source_target_pairs={{1,2},{3,4},{5,6},{7,0},{2,1},{4,3},{6,5},{0,7},{9,10},{11,12},{13... | collective-permute-start | bytes 786440 | tf_op jit(solution)/shard_map/ppermute | solution.py:349
  4.6 2.4 %smooth.1 = (bf16[2,32,8192]{2,1,0:T(8,128)(2,1)S(1)}, bf16[64,8192]{1,0:T(8,128)(2,1)S(1)}, f32[32,256]{1,0:T(8,128)S(1)}, f32[32,256]{1,0:T(8,128)S(1)}, f32[3...) custom-call(f32[9,256]{1,0:T(8,128)} %bitcast.8, ...), custom_call_target="tpu_custom_call" | custom-call | bytes 2097152 | tf_op jit(solution)/shard_map/smooth/pallas_call | solution.py:358
  7.0 1.2 %collective-permute-start = (bf16[16,8192]{1,0:T(8,128)(2,1)S(1)}, bf16[16,8192]{1,0:T(8,128)(2,1)S(1)}, u32[]{:S(2)}, u32[]{:S(2)}) collective-permute-start(bf16[16,8192]{1,0:T(8,128)(2,1)S(1)} %get-tuple-element.29), channel_id=1, source_target_pairs={{0,1},{1,0},{2,3},{3,2},{4,5},{5,4},{6,7},{7,6},{8,9},{9,8},{10,11... | collective-permute-start | bytes 786440 | tf_op jit(solution)/shard_map/ppermute | solution.py:381
  8.2 3.2 %interior.1 = (bf16[48,4,128,128]{3,2,1,0:T(8,128)(2,1)S(1)}, bf16[64,32,128]{2,1,0:T(8,128)(2,1)S(1)}) custom-call(s32[4,64]{1,0:T(4,128)S(1)} %get-tuple-element.21.table_ref, bf16[64,32,128]{2,1,0:T(8,128)(2,1)S(1)} %get-tuple-element.24.smooth_ref, bf16[16,4,128,128]{3,2,1,0:T(8,128)(2,1)S(1)} %get-tuple-element.23.early_ref, ...), custom_call_target="tpu_custom_call" | custom-call | flops 268435456 | bytes 16777216 | tf_op jit(solution)/shard_map/interior/pallas_call | solution.py:382
  11.4 0.0 collective-permute-done.1.link_ref
  11.4 0.0 collective-permute-done.chip_ref
  11.4 4.9 %product.1 = (bf16[64,32,128]{2,1,0:T(8,128)(2,1)S(1)}, bf16[8,32,256]{2,1,0:T(8,128)(2,1)S(1)}, bf16[8,32,256]{2,1,0:T(8,128)(2,1)S(1)}, bf16[8,32,256]{2,1,0:T(8,128)(2,1)S(1)}) custom-call(s32[4,64]{1,0:T(4,128)S(1)} %get-tuple-element.21.table_ref, bf16[96,96]{1,0:T(8,128)(2,1)S(1)} %get-tuple-element.27.band_ref, ...), custom_call_target="tpu_custom_call" | custom-call | tf_op jit(solution)/shard_map/product/pallas_call | solution.py:421
  16.3 1.3 %collective-permute-start.2 = (bf16[8,32,256]{2,1,0:T(8,128)(2,1)S(1)}, bf16[8,32,256]{2,1,0:T(8,128)(2,1)S(1)}, u32[]{:S(2)}, u32[]{:S(2)}) collective-permute-start(bf16[8,32,256]{2,1,0:T(8,128)(2,1)S(1)} %get-tuple-element.31), channel_id=1, source_target_pairs={{0,8},{8,16},{16,24},{24,0},{32,40},{40,48},{48,56},{56,32},{64,72... | collective-permute-start | bytes 393224 | tf_op jit(solution)/shard_map/ppermute | solution.py:418
  17.6 1.5 %collective-permute-start.3 = (bf16[8,32,256]{2,1,0:T(8,128)(2,1)S(1)}, bf16[8,32,256]{2,1,0:T(8,128)(2,1)S(1)}, u32[]{:S(2)}, u32[]{:S(2)}) collective-permute-start(bf16[8,32,256]{2,1,0:T(8,128)(2,1)S(1)} %get-tuple-element.32), channel_id=1, source_target_pairs={{0,24},{8,0},{16,8},{24,16},{32,56},{40,32},{48,40},{56,48},{64,88... | collective-permute-start | bytes 393224 | tf_op jit(solution)/shard_map/ppermute | solution.py:418
  19.2 1.6 %collective-permute-start.4 = (bf16[8,32,256]{2,1,0:T(8,128)(2,1)S(1)}, bf16[8,32,256]{2,1,0:T(8,128)(2,1)S(1)}, u32[]{:S(2)}, u32[]{:S(2)}) collective-permute-start(bf16[8,32,256]{2,1,0:T(8,128)(2,1)S(1)} %get-tuple-element.33), channel_id=1, source_target_pairs={{0,16},{8,24},{16,0},{24,8},{32,48},{40,56},{48,32},{56,40},{64,80... | collective-permute-start | bytes 393224 | tf_op jit(solution)/shard_map/ppermute | solution.py:418
  20.7 1.4 %own.1.own_ref = f32[8,32,256]{2,1,0:T(8,128)S(1)} custom-call(s32[4,64]{1,0:T(4,128)S(1)} %get-tuple-element.21.table_ref, bf16[2,32,8192]{2,1,0:T(8,128)(2,1)S(1)} %get-tuple-element.22.members_ref, bf16[16,4,128,128]{3,2,1,0:T(8,128)(2,1)S(1)} %get-tuple-element.23.early_ref, bf16[48,4,128,128]{3,2,1,0:T(8,128)(2,1)S(1)} %get-tuple-element.25.late_ref, ...), custom_call_target="tpu_custom_call" | custom-call | flops 134217728 | bytes 2097152 | tf_op jit(solution)/shard_map/own/pallas_call | solution.py:404
  22.2 0.0 collective-permute-done.2.refs_0_
  22.2 0.2 collective-permute-done.3.refs_1_
  22.4 3.8 %collective-permute-done.4.refs_2_ = bf16[8,32,256]{2,1,0:T(8,128)(2,1)S(1)} collective-permute-done((bf16[8,32,256]{2,1,0:T(8,128)(2,1)S(1)}, bf16[8,32,256]{2,1,0:T(8,128)(2,1)S(1)}, u32[]{:S(2)}, u32[]{:S(2)}) %collective-permute-start.4) | collective-permute-done | bytes 131104 | tf_op jit(solution)/shard_map/ppermute | solution.py:418
  26.2 0.1 fold.1
  26.3 16.2 %all_to_all.10.parts_ref = bf16[8,32,256]{2,1,0:T(8,128)(2,1)S(1)} all-to-all(bf16[8,32,256]{2,1,0:T(8,128)(2,1)S(1)} %fold.1), channel_id=1, replica_groups={{0,32,64,96,128,160,192,224},{8,40,72,104,136,168,200,232},{16,48,80,11..., dimensions={0} | all-to-all | bytes 262144 | tf_op jit(solution)/shard_map/all_to_all | solution.py:446
  42.5 0.2 image.1
  42.8 20.0 %all_to_all.11 = f32[256,1,128]{2,1,0:T(1,128)S(1)} all-to-all(f32[256,1,128]{2,1,0:T(1,128)S(1)} %bitcast.7), channel_id=1, replica_groups={{255,254,253,252,251,250,249,248,247,246,245,244,243,242,241,240,239,23..., dimensions={0} | all-to-all | bytes 262144 | tf_op jit(solution)/shard_map/all_to_all | solution.py:457
  62.8 1.2 %update.1 = (f32[32,256]{1,0:T(8,128)}, f32[32,256]{1,0:T(8,128)}, f32[32,256]{1,0:T(8,128)}) custom-call(f32[256,128]{1,0:T(8,128)S(1)} %bitcast.6, f32[32,256]{1,0:T(8,128)S(1)} %get-tuple-element.34.own_ref, f32[32,256]{1,0:T(8,128)S(1)} %get-tuple-element.35.residual_ref, f32[32,256]{1,0:T(8,128)S(1)} %get-tuple-element.37.iterate_ref, ...), custom_call_target="tpu_custom_call" | custom-call | tf_op jit(solution)/shard_map/update/pallas_call | solution.py:461
Async XLA Ops:
  1.9 9.5 %collective-permute-start.1 = (bf16[16,8192]{1,0:T(8,128)(2,1)S(1)}, bf16[16,8192]{1,0:T(8,128)(2,1)S(1)}, u32[]{:S(2)}, u32[]{:S(2)}) collective-permute-start(bf16[16,8192]{1,0:T(8,128)(2,1)S(1)} %link_edge.1), channel_id=1, source_target_pairs={{1,2},{3,4},{5,6},{7,0},{2,1},{4,3},{6,5},{0,7},{9,10},{11,12},{13... | collective-permute-start | bytes 786440 | tf_op jit(solution)/shard_map/ppermute | solution.py:349
  7.0 4.4 %collective-permute-start = (bf16[16,8192]{1,0:T(8,128)(2,1)S(1)}, bf16[16,8192]{1,0:T(8,128)(2,1)S(1)}, u32[]{:S(2)}, u32[]{:S(2)}) collective-permute-start(bf16[16,8192]{1,0:T(8,128)(2,1)S(1)} %get-tuple-element.29), channel_id=1, source_target_pairs={{0,1},{1,0},{2,3},{3,2},{4,5},{5,4},{6,7},{7,6},{8,9},{9,8},{10,11... | collective-permute-start | bytes 786440 | tf_op jit(solution)/shard_map/ppermute | solution.py:381
  16.3 5.9 %collective-permute-start.2 = (bf16[8,32,256]{2,1,0:T(8,128)(2,1)S(1)}, bf16[8,32,256]{2,1,0:T(8,128)(2,1)S(1)}, u32[]{:S(2)}, u32[]{:S(2)}) collective-permute-start(bf16[8,32,256]{2,1,0:T(8,128)(2,1)S(1)} %get-tuple-element.31), channel_id=1, source_target_pairs={{0,8},{8,16},{16,24},{24,0},{32,40},{40,48},{48,56},{56,32},{64,72... | collective-permute-start | bytes 393224 | tf_op jit(solution)/shard_map/ppermute | solution.py:418
  17.6 4.8 %collective-permute-start.3 = (bf16[8,32,256]{2,1,0:T(8,128)(2,1)S(1)}, bf16[8,32,256]{2,1,0:T(8,128)(2,1)S(1)}, u32[]{:S(2)}, u32[]{:S(2)}) collective-permute-start(bf16[8,32,256]{2,1,0:T(8,128)(2,1)S(1)} %get-tuple-element.32), channel_id=1, source_target_pairs={{0,24},{8,0},{16,8},{24,16},{32,56},{40,32},{48,40},{56,48},{64,88... | collective-permute-start | bytes 393224 | tf_op jit(solution)/shard_map/ppermute | solution.py:418
  19.2 7.1 %collective-permute-start.4 = (bf16[8,32,256]{2,1,0:T(8,128)(2,1)S(1)}, bf16[8,32,256]{2,1,0:T(8,128)(2,1)S(1)}, u32[]{:S(2)}, u32[]{:S(2)}) collective-permute-start(bf16[8,32,256]{2,1,0:T(8,128)(2,1)S(1)} %get-tuple-element.33), channel_id=1, source_target_pairs={{0,16},{8,24},{16,0},{24,8},{32,48},{40,56},{48,32},{56,40},{64,80... | collective-permute-start | bytes 393224 | tf_op jit(solution)/shard_map/ppermute | solution.py:418
